TPU v7x, 256 devices: a whole 4x4x8 slice. The times are simulated.
256 devices in a mesh: batch: 32 (over x, z), node: 4 (over y), replica: 2 (over core).
Axes of the slice: x: 4, y: 4, z: 8, core: 2. Of those that a mesh axis runs over, the one named last changes fastest.
Arguments:
- embed_table: bfloat16 [32768, 1024], P('batch'), may hold values from -6 to 6
- owner_shard: int32 [64, 256, 1], P(('batch', 'replica')), may hold values from 0 to 31; in each aligned block of 256 rows (0 to 255, 256 to 511, ..., all dimensions but the last counted through in order) at most 12 rows name the same one
- local_row: int32 [64, 256], P(('batch', 'replica')), may hold values from 0 to 1023
- lengths: int32 [64], P(('batch', 'replica')), may hold values from 64 to 256
- spd_bucket: int32 [64, 256, 256], P(('batch', 'replica')), may hold values from 0 to 15, as said below
- degree_bucket: int32 [64, 256], P(('batch', 'replica')), may hold values from 0 to 31, as said below
- w_query: bfloat16 [1024, 1024], P(None, 'node'), may hold values from -0.1875 to 0.1875
- w_key: bfloat16 [1024, 1024], P(None, 'node'), may hold values from -0.1875 to 0.1875
- w_value: bfloat16 [1024, 1024], P(None, 'node'), may hold values from -0.1875 to 0.1875
- w_out: bfloat16 [1024, 1024], P('node'), may hold values from -0.1875 to 0.1875
- spd_bias: float32 [16, 16], P(None, 'node'), may hold values from -4 to 4
- degree_bias: float32 [32, 16], P(None, 'node'), may hold values from -2 to 253
- cotangent: bfloat16 [64, 256, 1024], P(('batch', 'replica')), may hold values from -6 to 6
Outputs:
- table_grad: float32 [32768, 1024], P('batch', ('node', 'replica'))
- query_grad: float32 [1024, 1024], P(None, 'node')
- key_grad: float32 [1024, 1024], P(None, 'node')
- value_grad: float32 [1024, 1024], P(None, 'node')
- out_grad: float32 [1024, 1024], P('node')
- spd_grad: float32 [16, 16], P(None, 'node')
- degree_grad: float32 [32, 16], P(None, 'node')
Inputs may be any that keep to these rules, and one draw needn't show every extreme that they name: `owner_shard`: in each aligned block of 256 slots (the subgraphs of one index of batch and replica) no owner shard is named by more than 12 slots, a bound that some block reaches. `lengths`: slots at or past a subgraph's length are padding. `spd_bucket`: symmetric in its last two dimensions, 0 exactly on the diagonal. `degree_bucket`: some subgraphs hold only buckets below half of 32.
All inputs are finite; a program needn't handle non-finite values.
Results may differ from a plain program's by a relative error of at most 0.015.
Values may be sent and summed in bfloat16 or wider, within the bound.
A program may use at most 64 MiB of HBM per device.

v0:
```python
import jax
import jax.numpy as jnp
from jax import lax
from jax.sharding import PartitionSpec as P

HEAD_DIM = 64
NSPD = 16
NDEG = 32


EPS = 1e-05


def normalize(rows_in):
    widened = rows_in.astype(jnp.float32)
    mean_val = jnp.mean(widened, axis=-1, keepdims=True)
    centred = widened - mean_val
    inv_std = lax.rsqrt(jnp.mean(centred * centred, axis=-1, keepdims=True) + EPS)
    return (centred * inv_std, inv_std)


def on_device(
    embed_table,
    owner_shard,
    local_row,
    lengths,
    spd_bucket,
    degree_bucket,
    w_query,
    w_key,
    w_value,
    w_out,
    spd_bias,
    degree_bias,
    cotangent,
):
    group_count, slot_count, feature_dim = cotangent.shape
    slot_total = group_count * slot_count
    row_count = embed_table.shape[0]
    peer_count = lax.axis_size("batch")
    capacity = 3 * slot_total // (2 * peer_count)
    dest_shard = owner_shard.reshape(slot_total)
    wanted = local_row.reshape(slot_total)
    bucket_hits = (dest_shard[:, None] == jnp.arange(peer_count, dtype=jnp.int32)[None, :]).astype(
        jnp.int32
    )
    bucket_rank = jnp.sum((jnp.cumsum(bucket_hits, axis=0) - bucket_hits) * bucket_hits, axis=1)
    slot_place = dest_shard * capacity + bucket_rank
    requests = jnp.full((peer_count * capacity,), -1, jnp.int32).at[slot_place].set(wanted)
    asked_rows = lax.all_to_all(
        requests.reshape(peer_count, capacity), "batch", split_axis=0, concat_axis=0, tiled=True
    ).reshape(peer_count * capacity)
    present = asked_rows >= 0
    safe_rows = jnp.where(present, asked_rows, 0)
    target_rows = jnp.where(present, asked_rows, row_count)
    fetched = lax.all_to_all(
        embed_table[safe_rows].reshape(peer_count, capacity, feature_dim),
        "batch",
        split_axis=0,
        concat_axis=0,
        tiled=True,
    )
    slot_rows = fetched.reshape(peer_count * capacity, feature_dim)[slot_place]
    x_hat, inv_std = normalize(slot_rows)
    normed = x_hat.astype(jnp.bfloat16)
    local_width = w_query.shape[1]
    head_local = local_width // HEAD_DIM
    head_shape = (group_count, slot_count, head_local, HEAD_DIM)
    score_scale = HEAD_DIM ** (-0.5)

    def project(weight):
        return jnp.dot(normed, weight, preferred_element_type=jnp.float32).astype(jnp.bfloat16)

    queries = project(w_query).reshape(head_shape)
    key_rows = project(w_key).reshape(head_shape)
    values = project(w_value).reshape(head_shape)
    valid_slot = jnp.arange(slot_count, dtype=jnp.int32)[None, :] < lengths[:, None]
    spd_hot = (spd_bucket[..., None] == jnp.arange(NSPD, dtype=jnp.int32)).astype(jnp.float32)
    degree_hot = (degree_bucket[..., None] == jnp.arange(NDEG, dtype=jnp.int32)).astype(jnp.float32)
    spd_term = jnp.einsum("gijb,bh->ghij", spd_hot, spd_bias, precision=lax.Precision.HIGHEST)
    degree_term = jnp.einsum(
        "gjb,bh->ghj", degree_hot, degree_bias, precision=lax.Precision.HIGHEST
    )[:, :, None, :]
    scores = (
        jnp.einsum("gihd,gjhd->ghij", queries, key_rows, preferred_element_type=jnp.float32)
        * score_scale
        + spd_term
        + degree_term
    )
    scores = jnp.where(valid_slot[:, None, None, :], scores, -jnp.inf)
    row_top = jnp.max(scores, axis=-1, keepdims=True)
    exp_scores = jnp.exp(scores - row_top)
    probs = exp_scores / jnp.sum(exp_scores, axis=-1, keepdims=True)
    probs_b = probs.astype(jnp.bfloat16)
    attended = (
        jnp.einsum("ghij,gjhd->gihd", probs_b, values, preferred_element_type=jnp.float32)
        .astype(jnp.bfloat16)
        .reshape(slot_total, local_width)
    )
    d_masked = jnp.where(valid_slot[:, :, None], cotangent, jnp.zeros_like(cotangent)).reshape(
        slot_total, feature_dim
    )
    d_att = jnp.dot(d_masked, w_out.T, preferred_element_type=jnp.float32).astype(jnp.bfloat16)
    out_part = jnp.dot(attended.T, d_masked, preferred_element_type=jnp.float32)
    d_att_h = d_att.reshape(head_shape)
    d_values = (
        jnp.einsum("ghij,gihd->gjhd", probs_b, d_att_h, preferred_element_type=jnp.float32)
        .astype(jnp.bfloat16)
        .reshape(slot_total, local_width)
    )
    d_probs = jnp.einsum("gihd,gjhd->ghij", d_att_h, values, preferred_element_type=jnp.float32)
    d_scores = probs * (d_probs - jnp.sum(probs * d_probs, axis=-1, keepdims=True))
    spd_part = jnp.einsum("gijb,ghij->bh", spd_hot, d_scores, precision=lax.Precision.HIGHEST)
    degree_part = jnp.einsum("gjb,ghij->bh", degree_hot, d_scores, precision=lax.Precision.HIGHEST)
    d_scores_b = d_scores.astype(jnp.bfloat16)
    d_queries = (
        (
            jnp.einsum("ghij,gjhd->gihd", d_scores_b, key_rows, preferred_element_type=jnp.float32)
            * score_scale
        )
        .astype(jnp.bfloat16)
        .reshape(slot_total, local_width)
    )
    d_keys = (
        (
            jnp.einsum("ghij,gihd->gjhd", d_scores_b, queries, preferred_element_type=jnp.float32)
            * score_scale
        )
        .astype(jnp.bfloat16)
        .reshape(slot_total, local_width)
    )
    query_part = jnp.dot(normed.T, d_queries, preferred_element_type=jnp.float32)
    key_part = jnp.dot(normed.T, d_keys, preferred_element_type=jnp.float32)
    value_part = jnp.dot(normed.T, d_values, preferred_element_type=jnp.float32)
    d_normed = (
        jnp.dot(d_queries, w_query.T, preferred_element_type=jnp.float32)
        + jnp.dot(d_keys, w_key.T, preferred_element_type=jnp.float32)
        + jnp.dot(d_values, w_value.T, preferred_element_type=jnp.float32)
    )
    lead_flag = (lax.axis_index("node") == 0).astype(jnp.float32)
    d_rows = lead_flag * d_masked.astype(jnp.float32) + inv_std * (
        d_normed
        - jnp.mean(d_normed, axis=-1, keepdims=True)
        - x_hat * jnp.mean(d_normed * x_hat, axis=-1, keepdims=True)
    )
    send_back = (
        jnp.zeros((peer_count * capacity, feature_dim), jnp.float32).at[slot_place].set(d_rows)
    )
    returned = (
        lax.all_to_all(
            send_back.reshape(peer_count, capacity, feature_dim).astype(jnp.bfloat16),
            "batch",
            split_axis=0,
            concat_axis=0,
            tiled=True,
        )
        .astype(jnp.float32)
        .reshape(peer_count * capacity, feature_dim)
    )
    accum = (
        jnp.zeros((row_count, feature_dim), jnp.float32).at[target_rows].add(returned, mode="drop")
    )
    table_grad = lax.psum_scatter(
        accum.astype(jnp.bfloat16), ("node", "replica"), scatter_dimension=1, tiled=True
    ).astype(jnp.float32)
    summed = lax.psum(
        (query_part, key_part, value_part, out_part, spd_part, degree_part), ("batch", "replica")
    )
    copies = float(peer_count * lax.axis_size("replica"))
    return (
        table_grad,
        summed[0] / copies,
        summed[1] / copies,
        summed[2] / copies,
        summed[3] / copies,
        summed[4] / copies,
        summed[5] / copies,
    )


def solution(mesh):
    placed = (
        P("batch", None),
        P(("batch", "replica"), None, None),
        P(("batch", "replica"), None),
        P(("batch", "replica")),
        P(("batch", "replica"), None, None),
        P(("batch", "replica"), None),
        P(None, "node"),
        P(None, "node"),
        P(None, "node"),
        P("node", None),
        P(None, "node"),
        P(None, "node"),
        P(("batch", "replica"), None, None),
    )
    return jax.shard_map(
        on_device,
        mesh=mesh,
        in_specs=placed,
        out_specs=(
            P("batch", ("node", "replica")),
            P(None, "node"),
            P(None, "node"),
            P(None, "node"),
            P("node", None),
            P(None, "node"),
            P(None, "node"),
        ),
        check_vma=False,
    )
```

profile of v0, /device:TPU:1, one launch (start us, length us, event | category | flops | bytes accessed | tf_op | source)
XLA Modules:
  0.0 309.4 jit_solution(10417535351380792851)
XLA Ops:
  8.0 0.8 fusion.50
  8.8 0.6 reduce-window.6
  9.4 0.2 slice_reduce_fusion
  9.7 0.8 fusion.49
  10.4 0.7 compare_select_fusion.4
  11.1 1.6 scatter_custom_fusion
  12.8 20.3 %all_to_all.19 = s32[32,1,12]{2,1,0:T(1,128)S(1)} all-to-all(s32[32,1,12]{2,1,0:T(1,128)S(1)} %bitcast.120), channel_id=1, replica_groups=mesh['batch'=32,'node'=4,'replica'=2] {'batch'}, dimensions={0} | all-to-all | bytes 3072 | tf_op jit(solution)/shard_map/all_to_all | solution.py:50
  33.1 0.5 broadcast.245
  33.6 0.7 reduce.17
  34.3 0.1 reshape.325
  34.4 0.6 fusion.53
  35.0 2.1 gather_fusion
  37.1 1.1 reshape.327
  38.2 4.7 %all-to-all-start.1 = ((bf16[32,12,1024]{2,1,0:T(8,128)(2,1)}), bf16[32,12,1024]{2,1,0:T(8,128)(2,1)}, u32[]{:S(2)}, u32[]{:S(2)}) async-start(bf16[32,12,1024]{2,1,0:T(8,128)(2,1)} %reshape.327), calls=%async_computation.1 | async-start | bytes 2097152 | tf_op jit(solution)/shard_map/all_to_all | solution.py:56
  43.0 1.3 fusion.2
  44.3 1.4 copy.39
  46.4 0.2 convolution_bitcast_fusion
  46.6 2.3 convolution_convert_fusion.3
  48.9 18.4 %all-to-all-done.1 = bf16[32,12,1024]{2,1,0:T(8,128)(2,1)} async-done(((bf16[32,12,1024]{2,1,0:T(8,128)(2,1)}), bf16[32,12,1024]{2,1,0:T(8,128)(2,1)}, u32[]{:S(2)}, u32[]{:S(2)}) %all-to-all-start.1) | async-done | bytes 786464 | tf_op jit(solution)/shard_map/all_to_all | solution.py:56
  67.3 1.3 reshape.328
  68.6 1.2 gather_fusion.1
  69.8 0.1 convert_reduce_fusion
  70.0 0.3 fusion.26
  70.3 1.5 convolution_convert_fusion.5
  71.8 0.5 convolution_convert_fusion.4
  72.3 0.4 fusion.11
  72.7 0.8 fusion.67
  73.4 0.5 convolution_convert_fusion.2
  73.9 0.4 multiply_reduce_fusion
  74.3 0.2 fusion.66
  74.5 0.2 fusion.17
  74.7 0.8 copy-done.1
  75.5 0.3 fusion.18
  75.8 1.9 convolution_convert_fusion.1
  77.7 2.4 fusion.68
  80.1 1.4 fusion.60
  81.5 1.9 convolution_convert_fusion
  83.5 1.5 fusion.58
  84.9 1.5 fusion.56
  86.4 1.4 fusion.31
  87.8 0.2 reduce-scatter.4.cloned.1.call-start
  88.0 1.8 convolution_add_fusion.1
  89.8 1.4 fusion.65
  91.3 3.8 %scatter_custom_fusion.1 = f32[384,1024]{1,0:T(8,128)} fusion(s32[256]{0:T(256)} %bitcast.125, bf16[256,1024]{1,0:T(8,128)(2,1)S(1)} %gather_fusion.1, f32[256,1024]{1,0:T(8,128)} %get-tuple-element.23, f32[]{:T(128)} %constant.15.clone.1, f32[256]{0:T(256)S(1)} %get-tuple-element.24, f32[256]{0:T(256)S(1)} %get-tuple-element.25, ...), kind=kCustom, calls=%fused_computation.44 | custom fusion | flops 2883584 | bytes 3674884 | tf_op jit(solution)/shard_map/scatter | solution.py:147
  95.0 2.4 convert_element_type.111
  97.4 1.2 convert_element_type.112
  98.7 36.8 %all_to_all.20 = bf16[32,12,1024]{2,1,0:T(8,128)(2,1)} all-to-all(bf16[32,12,1024]{2,1,0:T(8,128)(2,1)S(1)} %convert_element_type.112), channel_id=1, replica_groups=mesh['batch'=32,'node'=4,'replica'=2] {'batch'}, dimensions={0} | all-to-all | bytes 1572864 | tf_op jit(solution)/shard_map/all_to_all | solution.py:150
  135.4 2.4 reshape.377
  137.8 6.7 %scatter_custom_fusion.2 = f32[1024,1024]{1,0:T(8,128)} fusion(s32[384]{0:T(512)} %get-tuple-element.10, f32[384,1024]{1,0:T(8,128)} %reshape.377, f32[]{:T(128)} %constant.15.clone.1), kind=kCustom, calls=%fused_computation.11 | custom fusion | flops 393216 | bytes 4194816 | tf_op jit(solution)/shard_map/scatter-add | solution.py:161
  144.5 3.9 %convert_element_type.113 = bf16[1024,1024]{1,0:T(8,128)(2,1)} convert(f32[1024,1024]{1,0:T(8,128)} %scatter_custom_fusion.2) | non-fusion elementwise | flops 1048576 | bytes 6291456 | tf_op jit(solution)/shard_map/convert_element_type | solution.py:164
  148.4 4.0 %copy.52 = bf16[1024,1024]{0,1:T(8,128)(2,1)} copy(bf16[1024,1024]{1,0:T(8,128)(2,1)} %convert_element_type.113) | data formatting | bytes 4194304
  152.4 1.2 copy-done.2
  153.6 1.3 copy.46
  154.9 4.0 %fusion.19 = f32[16,4]{0,1:T(4,128)S(1)} fusion(f32[4,256,256]{2,0,1:T(4,128)} %copy.46, s32[256,256]{1,0:T(8,128)S(1)} %bitcast.117), kind=kOutput, calls=%fused_computation.39 | convolution fusion | flops 51380224 | bytes 1310976 | tf_op jit(solution)/shard_map/gijb,ghij->bh/dot_general | solution.py:113
  158.9 0.2 fusion.44
  159.1 127.5 %all-reduce = (f32[16,4]{0,1:T(4,128)S(1)}, f32[32,4]{0,1:T(4,128)S(1)}) all-reduce(f32[16,4]{0,1:T(4,128)S(1)} %fusion.19, f32[32,4]{0,1:T(4,128)S(1)} %fusion.44), channel_id=1, replica_groups=mesh['batch'=32,'node'=4,'replica'=2] {'batch','replica'}, use_global_device_ids=true, to_apply=%region_18.19 | all-reduce | flops 192 | bytes 1536 | tf_op jit(solution)/shard_map/psum | solution.py:166
  286.6 0.6 broadcast_multiply_fusion.5
  287.2 0.6 broadcast_multiply_fusion.4
  287.7 7.2 %all-reduce.4.cloned.1.call-done = (f32[1024,256]{1,0:T(8,128)}, f32[1024,256]{1,0:T(8,128)}, f32[1024,256]{1,0:T(8,128)}, f32[256,1024]{1,0:T(8,128)}) async-done(((f32[1024,256]{1,0:T(8,128)}, f32[1024,256]{1,0:T(8,128)}, f32[1024,256]{1,0:T(8,128)}, f32[256,1024]{1,0:T(8,128)}), (f32[1024,256]{1,0:T(8,128)}, f32[1024,256]{1,0:T(8,128)}, f32[1024,256]{1,0:T(8,128)}, ...) | async-done | bytes 4194320 | tf_op jit(solution)/shard_map/psum | solution.py:166
  295.0 2.4 broadcast_multiply_fusion.3
  297.4 1.1 broadcast_multiply_fusion
  298.5 1.5 broadcast_multiply_fusion.1
  300.0 1.1 copy.53
  301.1 0.8 convert_element_type.114
  (51 shorter events, 0.4 us)
Async XLA Ops:
  8.0 27.0 %copy-start = (bf16[1024,1024]{1,0:T(8,128)(2,1)S(1)}, bf16[1024,1024]{1,0:T(8,128)(2,1)}, u32[]{:S(2)}) copy-start(bf16[1024,1024]{1,0:T(8,128)(2,1)} %param.13) | copy-start | bytes 6291460
  11.1 35.2 %copy-start.14 = (s32[256,1]{0,1:T(1,128)}, s32[256,1]{0,1:T(1,128)S(1)}, u32[]{:S(2)}) copy-start(s32[256,1]{0,1:T(1,128)S(1)} %compare_select_fusion.4) | copy-start | bytes 3076
  37.1 5.9 %copy-start.12 = (s32[1,256,256]{2,1,0:T(8,128)S(1)}, s32[1,256,256]{2,1,0:T(8,128)}, u32[]{:S(2)}) copy-start(s32[1,256,256]{2,1,0:T(8,128)} %param.17) | copy-start | bytes 786436
  37.1 5.9 %copy-start.15 = (f32[16,4]{0,1:T(4,128)S(1)}, f32[16,4]{0,1:T(4,128)}, u32[]{:S(2)}) copy-start(f32[16,4]{0,1:T(4,128)} %param.23) | copy-start | bytes 772
  38.2 29.0 %all-to-all-start.1 = ((bf16[32,12,1024]{2,1,0:T(8,128)(2,1)}), bf16[32,12,1024]{2,1,0:T(8,128)(2,1)}, u32[]{:S(2)}, u32[]{:S(2)}) async-start(bf16[32,12,1024]{2,1,0:T(8,128)(2,1)} %reshape.327), calls=%async_computation.1 | async-start | bytes 2097152 | tf_op jit(solution)/shard_map/all_to_all | solution.py:56
  42.9 3.4 %copy-start.16 = (f32[32,4]{0,1:T(4,128)S(1)}, f32[32,4]{0,1:T(4,128)}, u32[]{:S(2)}) copy-start(f32[32,4]{0,1:T(4,128)} %param.24) | copy-start | bytes 1540
  42.9 3.4 %copy-start.17 = (s32[1,256]{1,0:T(1,128)S(1)}, s32[1,256]{1,0:T(1,128)}, u32[]{:S(2)}) copy-start(s32[1,256]{1,0:T(1,128)} %param.18) | copy-start | bytes 3076
  42.9 252.0 %all-reduce.4.cloned.1.call-start = ((), (), s32[]{:S(2)}) async-start(), calls=%async_computation.5 | async-start | bytes 8388608 | tf_op jit(solution)/shard_map/psum | solution.py:166
  69.8 2.0 copy-start.11
  69.8 2.4 copy-start.3
  72.3 1.2 copy-start.9
  72.6 1.6 copy-start.4
  72.7 1.3 copy-start.19
  74.5 1.0 copy-start.1
  83.5 2.9 copy-start.5
  87.8 212.2 %reduce-scatter.4.cloned.1.call-start = ((), (), s32[]{:S(2)}) async-start(), calls=%async_computation.4 | async-start | bytes 2359296
  88.0 1.8 copy-start.10
  152.3 1.2 copy-start.2
  152.4 2.5 copy-start.13
  153.6 5.3 %copy-start.18 = (s32[1,256]{1,0:T(1,128)S(1)}, s32[1,256]{1,0:T(1,128)}, u32[]{:S(2)}) copy-start(s32[1,256]{1,0:T(1,128)} %param.18) | copy-start | bytes 3076
  295.0 2.4 copy-start.6
  295.0 3.5 %copy-start.7 = (f32[1024,256]{1,0:T(8,128)S(1)}, f32[1024,256]{1,0:T(8,128)}, u32[]{:S(2)}) copy-start(f32[1024,256]{1,0:T(8,128)} %get-tuple-element.14) | copy-start | bytes 3145732
  295.0 3.5 %copy-start.8 = (f32[1024,256]{1,0:T(8,128)S(1)}, f32[1024,256]{1,0:T(8,128)}, u32[]{:S(2)}) copy-start(f32[1024,256]{1,0:T(8,128)} %get-tuple-element.15) | copy-start | bytes 3145732
Sparse Core Ops, SparseCore 0:
  87.9 207.0 all-reduce.3
Sparse Core Ops, SparseCore 1:
  152.5 37.0 reduce-scatter.3
where the time goes:
time: 311 us; the launch traced here: 309 us
  blocking collectives  185 us (59%)
  other arithmetic  29.4 us (9%)
  matrix products  26.8 us (9%)
  waiting for transfers between devices  25.7 us (8%)
  local copies, waits for them, and re-layouts  21.6 us (7%)
  between operations  16.5 us (5%)
  starting transfers between devices  4.93 us (2%)
    psum x1, blocking collectives, on_device(): lax.psum((query_part, key_part, value_part, out_part, spd_part, degree_pa...  127 us
    all_to_all x1, blocking collectives, on_device(): lax.all_to_all(send_back.reshape(peer_count, capacity, feature_dim).astyp...  36.8 us
    all_to_all x1, blocking collectives, on_device(): lax.all_to_all(requests.reshape(peer_count, capacity), 'batch', split_axi...  20.3 us
    all_to_all x1, waiting for transfers between devices, on_device(): lax.all_to_all(embed_table[safe_rows].reshape(peer_count, capacity, featu...  18.4 us
    psum x1, waiting for transfers between devices, on_device(): lax.psum((query_part, key_part, value_part, out_part, spd_part, degree_pa...  7.24 us
    unnamed x42, local copies, waits for them, and re-layouts  7.14 us
    scatter-add x1, other arithmetic, on_device(): jnp.zeros((row_count, feature_dim), jnp.float32).at[target_rows]  6.66 us
  transfers between devices with their start and end apart: 3, of which 2 were waited for; matrix products, arithmetic and copies ran while one was open for 14% of the time, Pallas kernels for 0%

commit v1 on v0

v1 whole, which is shorter than its diff:
```python
import functools

import jax
import jax.numpy as jnp
from jax import lax
from jax.experimental import pallas as pl
from jax.experimental.pallas import tpu as pltpu
from jax.sharding import PartitionSpec as P

HEAD_DIM = 64
NSPD = 16
NDEG = 32
EPS = 1e-05
PAIR_ROWS = 16
Z_SIZE = 8
MESH = pl.DeviceIdType.MESH
F32 = jnp.float32
BF16 = jnp.bfloat16
I32 = jnp.int32


def iota(shape, dim):
    return lax.broadcasted_iota(I32, shape, dim)


def dot(a, b, ca=1, cb=0, precision=None):
    return lax.dot_general(
        a, b, (((ca,), (cb,)), ((), ())), preferred_element_type=F32, precision=precision
    )


def remote(src, dst, send_sem, recv_sem, **where):
    return pltpu.make_async_remote_copy(
        src_ref=src,
        dst_ref=dst,
        send_sem=send_sem,
        recv_sem=recv_sem,
        device_id=where,
        device_id_type=MESH,
    )


def wait_bytes(ref, sem):
    pltpu.make_async_copy(ref, ref, sem).wait()


def greet(batch, nodes, n_batch, n_node):
    me_b, me_n, me_r = lax.axis_index("batch"), lax.axis_index("node"), lax.axis_index("replica")
    barrier = pltpu.get_barrier_semaphore()

    if batch:

        def body(j, carry):
            pl.semaphore_signal(
                barrier, inc=1, device_id={"batch": lax.rem(me_b + j, n_batch)}, device_id_type=MESH
            )
            return carry

        lax.fori_loop(1, n_batch, body, 0)
    if nodes:
        for j in range(1, n_node):
            pl.semaphore_signal(
                barrier, inc=1, device_id={"node": lax.rem(me_n + j, n_node)}, device_id_type=MESH
            )
    pl.semaphore_signal(barrier, inc=1, device_id={"replica": 1 - me_r}, device_id_type=MESH)
    pl.semaphore_wait(barrier, (n_batch - 1) * batch + (n_node - 1) * nodes + 1)


def fetch_kernel(
    n_batch,
    n_node,
    owner_ref,
    local_ref,
    table_ref,
    rows_ref,
    reqs_ref,
    dest_ref,
    table_v,
    ask,
    spread,
    rows_send,
    rows_recv,
    local_sem,
    ssem,
    rsem,
):
    me_b, me_n, me_r = lax.axis_index("batch"), lax.axis_index("node"), lax.axis_index("replica")
    slots = owner_ref.shape[1]
    width = table_v.shape[1]
    table_rows = table_v.shape[0]
    entries = n_batch * PAIR_ROWS
    load = pltpu.make_async_copy(
        table_ref.at[:, pl.ds(pl.multiple_of(me_n * width, width), width)], table_v, local_sem
    )
    load.start()

    owner_row = owner_ref[...]
    across = jnp.broadcast_to(owner_row, (slots, slots))
    down = jnp.transpose(across)
    same = across == down
    r0, r1 = iota((slots, slots), 0), iota((slots, slots), 1)
    rank_row = jnp.sum(jnp.where(same & (r0 < r1), 1.0, 0.0), axis=0, keepdims=True).astype(I32)
    rank_col = jnp.sum(jnp.where(same & (r1 < r0), 1.0, 0.0), axis=1, keepdims=True).astype(I32)
    dest_ref[...] = owner_row * PAIR_ROWS + rank_row
    dest_col = down[:, 0:1] * PAIR_ROWS + rank_col

    wanted = local_ref[...] + 1
    hit = owner_row == iota((n_batch, slots), 0)
    high = jnp.where(hit, (wanted // 32).astype(F32), 0.0).astype(BF16)
    low = jnp.where(hit, (wanted % 32).astype(F32), 0.0).astype(BF16)
    at_rank = jnp.where(rank_col == iota((slots, 128), 1), 1.0, 0.0).astype(BF16)
    listed = (dot(high, at_rank) * 32.0 + dot(low, at_rank)).astype(I32)
    for o in range(n_batch):
        ask[o] = listed[o : o + 1, :]

    greet(True, True, n_batch, n_node)

    def send_ask(j, carry):
        p = lax.rem(me_b + j, n_batch)
        remote(ask.at[p], reqs_ref.at[me_r, me_b], ssem.at[0], rsem.at[0], batch=p).start()
        return carry

    lax.fori_loop(1, n_batch, send_ask, 0)
    reqs_ref[me_r, me_b] = ask[me_b]
    load.wait()
    wait_bytes(ask.at[pl.ds(0, n_batch - 1)], rsem.at[0])
    remote(
        reqs_ref.at[me_r], reqs_ref.at[me_r], ssem.at[1], rsem.at[1], replica=1 - me_r
    ).start()

    for p in range(n_batch):
        spread[p * PAIR_ROWS : (p + 1) * PAIR_ROWS, :] = jnp.broadcast_to(
            reqs_ref[me_r, p], (PAIR_ROWS, 128)
        )
    mine = iota((entries, 128), 1) == iota((entries, 128), 0) % PAIR_ROWS
    target = (
        jnp.sum(jnp.where(mine, spread[...].astype(F32), 0.0), axis=1, keepdims=True).astype(I32) - 1
    )
    pick = jnp.where(iota((entries, table_rows), 1) == target, 1.0, 0.0).astype(BF16)
    rows_send[...] = (
        dot(pick, table_v[...]).astype(BF16).reshape(n_batch, PAIR_ROWS, width)
    )

    def send_rows(j, carry):
        p = lax.rem(me_b + j, n_batch)
        remote(rows_send.at[p], rows_recv.at[me_b], ssem.at[2], rsem.at[2], batch=p).start()
        return carry

    lax.fori_loop(1, n_batch, send_rows, 0)
    rows_recv[me_b] = rows_send[me_b]
    place = jnp.where(iota((slots, entries), 1) == dest_col, 1.0, 0.0).astype(BF16)
    wait_bytes(rows_recv.at[pl.ds(0, n_batch - 1)], rsem.at[2])
    rows_ref[me_n] = dot(place, rows_recv[...].reshape(entries, width)).astype(BF16)
    for j in range(1, n_node):
        remote(
            rows_ref.at[me_n],
            rows_ref.at[me_n],
            ssem.at[3],
            rsem.at[3],
            node=lax.rem(me_n + j, n_node),
        ).start()
    wait_bytes(rows_ref.at[pl.ds(0, n_node - 1)], rsem.at[3])
    wait_bytes(reqs_ref.at[0], rsem.at[1])
    wait_bytes(ask.at[pl.ds(0, n_batch - 1)], ssem.at[0])
    wait_bytes(reqs_ref.at[0], ssem.at[1])
    wait_bytes(rows_send.at[pl.ds(0, n_batch - 1)], ssem.at[2])
    wait_bytes(rows_ref.at[pl.ds(0, n_node - 1)], ssem.at[3])


def layer_kernel(
    length_ref,
    spd_bias_ref,
    deg_bias_ref,
    rows_ref,
    spd_ref,
    deg_ref,
    cot_ref,
    wq_ref,
    wk_ref,
    wv_ref,
    wo_ref,
    grads_ref,
    d_rows_ref,
    small_ref,
    bias,
    d_scores,
    sums,
):
    slots, feature_dim = cot_ref.shape
    width = wq_ref.shape[1]
    heads = width // HEAD_DIM
    blocks = feature_dim // width
    length = length_ref[0]
    scale = HEAD_DIM ** (-0.5)
    step = 32

    def bias_block(i, carry):
        rows = pl.ds(pl.multiple_of(i * step, step), step)
        bucket = spd_ref[rows, :]
        terms = [jnp.full(bucket.shape, spd_bias_ref[0, h], F32) for h in range(heads)]
        for b in range(1, NSPD):
            is_b = bucket == b
            terms = [jnp.where(is_b, spd_bias_ref[b, h], terms[h]) for h in range(heads)]
        for h in range(heads):
            bias[h, rows, :] = terms[h]
        return carry

    lax.fori_loop(0, slots // step, bias_block, 0)
    degree = deg_ref[...]
    deg_terms = []
    for h in range(heads):
        term = jnp.full(degree.shape, deg_bias_ref[0, h], F32)
        for b in range(1, NDEG):
            term = jnp.where(degree == b, deg_bias_ref[b, h], term)
        deg_terms.append(term)

    cot = cot_ref[...]
    d_masked = jnp.where(iota((slots, feature_dim), 0) < length, cot.astype(F32), 0.0).astype(BF16)
    d_att = dot(d_masked, wo_ref[...], 1, 1).astype(BF16)

    x = jnp.concatenate([rows_ref[b] for b in range(blocks)], axis=1).astype(F32)
    centred = x - jnp.mean(x, axis=1, keepdims=True)
    inv_std = lax.rsqrt(jnp.mean(centred * centred, axis=1, keepdims=True) + EPS)
    x_hat = centred * inv_std
    normed = x_hat.astype(BF16)
    queries = dot(normed, wq_ref[...]).astype(BF16)
    keys = dot(normed, wk_ref[...]).astype(BF16)
    values = dot(normed, wv_ref[...]).astype(BF16)

    lane_head = iota((slots, width), 1) // HEAD_DIM

    def only(h, a):
        return jnp.where(lane_head == h, a, jnp.zeros_like(a))

    valid = iota((slots, slots), 1) < length
    attended = jnp.zeros((slots, width), F32)
    d_values = jnp.zeros((slots, width), F32)
    d_queries = jnp.zeros((slots, width), F32)
    d_keys = jnp.zeros((slots, width), F32)
    for h in range(heads):
        q_h, k_h, v_h, da_h = only(h, queries), only(h, keys), only(h, values), only(h, d_att)
        scores = dot(q_h, keys, 1, 1) * scale + bias[h] + deg_terms[h]
        scores = jnp.where(valid, scores, -jnp.inf)
        exps = jnp.exp(scores - jnp.max(scores, axis=1, keepdims=True))
        probs = exps / jnp.sum(exps, axis=1, keepdims=True)
        probs_b = probs.astype(BF16)
        attended = attended + dot(probs_b, v_h)
        d_values = d_values + dot(probs_b, da_h, 0, 0)
        d_probs = dot(da_h, values, 1, 1)
        ds = probs * (d_probs - jnp.sum(probs * d_probs, axis=1, keepdims=True))
        d_scores[h] = ds
        ds_b = ds.astype(BF16)
        d_queries = d_queries + dot(ds_b, k_h)
        d_keys = d_keys + dot(ds_b, q_h, 0, 0)
    attended = attended.astype(BF16)
    d_queries = (d_queries * scale).astype(BF16)
    d_keys = (d_keys * scale).astype(BF16)
    d_values = d_values.astype(BF16)

    halves = (2, 4, feature_dim // 8, width)
    out_part = dot(attended, d_masked, 0, 0).astype(BF16)
    for b in range(blocks):
        for k in range(2):
            grads_ref[0, b // 2, 2 * (b % 2) + k] = out_part[
                k * 128 : (k + 1) * 128, b * width : (b + 1) * width
            ]
    normed_t = jnp.transpose(normed)
    grads_ref[1] = dot(normed_t, d_values).astype(BF16).reshape(halves)
    grads_ref[2] = dot(normed_t, d_keys).astype(BF16).reshape(halves)
    grads_ref[3] = dot(normed_t, d_queries).astype(BF16).reshape(halves)

    d_normed = (
        dot(d_queries, wq_ref[...], 1, 1)
        + dot(d_keys, wk_ref[...], 1, 1)
        + dot(d_values, wv_ref[...], 1, 1)
    )
    lead = jnp.where(lax.axis_index("node") == 0, 1.0, 0.0)
    d_rows = lead * d_masked.astype(F32) + inv_std * (
        d_normed
        - jnp.mean(d_normed, axis=1, keepdims=True)
        - x_hat * jnp.mean(d_normed * x_hat, axis=1, keepdims=True)
    )
    for b in range(blocks):
        d_rows_ref[b] = d_rows[:, b * width : (b + 1) * width].astype(BF16)

    per_head = NSPD + NDEG
    sums[...] = jnp.zeros_like(sums)
    for h in range(heads):

        def spd_block(i, totals):
            rows = pl.ds(pl.multiple_of(i * step, step), step)
            bucket, ds = spd_ref[rows, :], d_scores[h, rows, :]
            new = []
            for b in range(NSPD):
                kept = jnp.where(bucket == b, ds, 0.0)
                kept = kept[:, :128] + kept[:, 128:]
                new.append(
                    totals[b] + (kept[0:8] + kept[8:16]) + (kept[16:24] + kept[24:32])
                )
            return tuple(new)

        totals = lax.fori_loop(
            0, slots // step, spd_block, tuple(jnp.zeros((8, 128), F32) for _ in range(NSPD))
        )
        for b in range(NSPD):
            at = h * per_head + b
            sums[at : at + 1, :] = jnp.sum(totals[b], axis=0, keepdims=True)
        by_key = jnp.sum(d_scores[h], axis=0, keepdims=True)
        kept = jnp.where(degree == iota((NDEG, slots), 0), by_key, 0.0)
        at = h * per_head + NSPD
        sums[at : at + NDEG, :] = kept[:, :128] + kept[:, 128:]
    small_ref[...] = dot(
        jnp.ones((8, 128), F32), sums[...], 1, 1, precision=lax.Precision.HIGHEST
    )


def reduce_kernel(
    n_batch,
    n_node,
    grads_ref,
    d_rows_ref,
    small_ref,
    dest_ref,
    reqs_ref,
    out_ref,
    table_ref,
    small_out,
    core_in,
    core_sum,
    x_in,
    x_sum,
    z_in,
    y_in,
    pack,
    to_core,
    table_in,
    small_core,
    small_x,
    small_z,
    spread,
    ssem,
    rsem,
    fs,
    fr,
    ts,
    tr,
):
    me_b, me_n, me_r = lax.axis_index("batch"), lax.axis_index("node"), lax.axis_index("replica")
    n_z = Z_SIZE
    n_x = n_batch // n_z
    me_x, me_z = me_b // n_z, me_b % n_z
    other = 1 - me_r
    chunks = grads_ref.shape[0]
    slots = dest_ref.shape[1]
    width = d_rows_ref.shape[2]
    half = width // 2
    entries = n_batch * PAIR_ROWS
    copies = 2.0 * n_batch
    piece = x_sum.shape[2]

    greet(True, True, n_batch, n_node)

    for j in range(1, n_node):
        p = lax.rem(me_n + j, n_node)
        remote(d_rows_ref.at[p], y_in.at[me_n], fs.at[0], fr.at[0], node=p).start()
    for c in range(chunks):
        remote(
            grads_ref.at[c, other], core_in.at[c], ssem.at[0, c], rsem.at[0, c], replica=other
        ).start()
    remote(small_ref, small_core, ts.at[0], tr.at[0], replica=other).start()
    y_in[me_n] = d_rows_ref[me_n]

    for c in range(chunks):
        wait_bytes(core_in.at[c], rsem.at[0, c])
        core_sum[c] = (grads_ref[c, me_r].astype(F32) + core_in[c].astype(F32)).astype(BF16)
        for j in range(1, n_x):
            p = lax.rem(me_x + j, n_x)
            remote(
                core_sum.at[c, p],
                x_in.at[c, me_x],
                ssem.at[1, c],
                rsem.at[1, c],
                batch=p * n_z + me_z,
            ).start()
        x_in[c, me_x] = core_sum[c, me_x]

    wait_bytes(small_core, tr.at[0])
    small_x[me_x] = small_ref[...] + small_core[...]
    for j in range(1, n_x):
        p = lax.rem(me_x + j, n_x)
        remote(
            small_x.at[me_x], small_x.at[me_x], ts.at[1], tr.at[1], batch=p * n_z + me_z
        ).start()

    place = jnp.where(iota((entries, slots), 0) == dest_ref[...], 1.0, 0.0).astype(BF16)
    wait_bytes(y_in.at[pl.ds(0, n_node - 1)], fr.at[0])
    d_rows = y_in[0].astype(F32)
    for n in range(1, n_node):
        d_rows = d_rows + y_in[n].astype(F32)
    packed = dot(place, d_rows.astype(BF16)).astype(BF16)
    left, right = packed[:, :half], packed[:, half:]
    shape = (n_batch, PAIR_ROWS, half)
    pack[me_r] = jnp.where(me_r == 0, left, right).reshape(shape)
    to_core[...] = jnp.where(me_r == 0, right, left).reshape(shape)
    remote(to_core, pack.at[me_r], fs.at[1], fr.at[1], replica=other).start()

    for c in range(chunks):
        wait_bytes(x_in.at[c, pl.ds(0, n_x - 1)], rsem.at[1, c])
        total = x_in[c, 0].astype(F32)
        for x in range(1, n_x):
            total = total + x_in[c, x].astype(F32)
        x_sum[c] = total.astype(BF16).reshape(n_z, piece, width)
        for j in range(1, n_z):
            p = lax.rem(me_z + j, n_z)
            remote(
                x_sum.at[c, p],
                z_in.at[c, me_z],
                ssem.at[2, c],
                rsem.at[2, c],
                batch=me_x * n_z + p,
            ).start()
        z_in[c, me_z] = x_sum[c, me_z]

    wait_bytes(small_x.at[pl.ds(0, n_x - 1)], tr.at[1])
    total = small_x[0]
    for x in range(1, n_x):
        total = total + small_x[x]
    small_z[me_z] = total
    for j in range(1, n_z):
        p = lax.rem(me_z + j, n_z)
        remote(
            small_z.at[me_z], small_z.at[me_z], ts.at[2], tr.at[2], batch=me_x * n_z + p
        ).start()

    wait_bytes(to_core, fr.at[1])

    def send_pack(j, carry):
        p = lax.rem(me_b + j, n_batch)
        remote(pack.at[:, p], table_in.at[:, me_b], fs.at[2], fr.at[2], batch=p).start()
        return carry

    lax.fori_loop(1, n_batch, send_pack, 0)
    table_in[:, me_b] = pack[:, me_b]

    for c in range(chunks):
        wait_bytes(z_in.at[c, pl.ds(0, n_z - 1)], rsem.at[2, c])
        total = z_in[c, 0].astype(F32)
        for z in range(1, n_z):
            total = total + z_in[c, z].astype(F32)
        out_ref[c, me_r, me_x, me_z] = (total * (1.0 / copies)).astype(BF16)
        for j in range(1, n_z):
            p = lax.rem(me_z + j, n_z)
            mine = out_ref.at[c, me_r, me_x, me_z]
            remote(mine, mine, ssem.at[3, c], rsem.at[3, c], batch=me_x * n_z + p).start()

    mine = iota((entries, 128), 1) == iota((entries, 128), 0) % PAIR_ROWS
    targets = []
    for r in range(2):
        for p in range(n_batch):
            spread[p * PAIR_ROWS : (p + 1) * PAIR_ROWS, :] = jnp.broadcast_to(
                reqs_ref[r, p], (PAIR_ROWS, 128)
            )
        target = jnp.sum(jnp.where(mine, spread[...].astype(F32), 0.0), axis=1, keepdims=True) - 1.0
        flat = jnp.transpose(jnp.broadcast_to(target, (entries, 128)))[0:1, :].astype(I32)
        targets.append(flat)

    for c in range(chunks):
        wait_bytes(out_ref.at[c, 0, 0, pl.ds(0, n_z - 1)], rsem.at[3, c])
        for j in range(1, n_x):
            p = lax.rem(me_x + j, n_x)
            mine = out_ref.at[c, me_r, me_x]
            remote(mine, mine, ssem.at[4, c], rsem.at[4, c], batch=p * n_z + me_z).start()

    wait_bytes(small_z.at[pl.ds(0, n_z - 1)], tr.at[2])
    total = small_z[0]
    for z in range(1, n_z):
        total = total + small_z[z]
    small_out[...] = total * (1.0 / copies)

    table_rows = table_ref.shape[0]
    row = iota((table_rows, entries), 0)
    scatter = [jnp.where(row == t, 1.0, 0.0).astype(BF16) for t in targets]
    wait_bytes(table_in.at[:, pl.ds(0, n_batch - 1)], fr.at[2])
    table_ref[...] = dot(scatter[0], table_in[0].reshape(entries, half)) + dot(
        scatter[1], table_in[1].reshape(entries, half)
    )

    for c in range(chunks):
        wait_bytes(out_ref.at[c, 0, pl.ds(0, n_x - 1)], rsem.at[4, c])
        mine = out_ref.at[c, me_r]
        remote(mine, mine, ssem.at[5, c], rsem.at[5, c], replica=other).start()
    for c in range(chunks):
        wait_bytes(out_ref.at[c, 0], rsem.at[5, c])

    wait_bytes(y_in.at[pl.ds(0, n_node - 1)], fs.at[0])
    wait_bytes(to_core, fs.at[1])
    wait_bytes(table_in.at[:, pl.ds(0, n_batch - 1)], fs.at[2])
    wait_bytes(small_core, ts.at[0])
    wait_bytes(small_x.at[pl.ds(0, n_x - 1)], ts.at[1])
    wait_bytes(small_z.at[pl.ds(0, n_z - 1)], ts.at[2])
    for c in range(chunks):
        wait_bytes(core_in.at[c], ssem.at[0, c])
        wait_bytes(x_in.at[c, pl.ds(0, n_x - 1)], ssem.at[1, c])
        wait_bytes(z_in.at[c, pl.ds(0, n_z - 1)], ssem.at[2, c])
        wait_bytes(out_ref.at[c, 0, 0, pl.ds(0, n_z - 1)], ssem.at[3, c])
        wait_bytes(out_ref.at[c, 0, pl.ds(0, n_x - 1)], ssem.at[4, c])
        wait_bytes(out_ref.at[c, 0], ssem.at[5, c])


def on_device(
    embed_table,
    owner_shard,
    local_row,
    lengths,
    spd_bucket,
    degree_bucket,
    w_query,
    w_key,
    w_value,
    w_out,
    spd_bias,
    degree_bias,
    cotangent,
):
    n_batch, n_node = lax.axis_size("batch"), lax.axis_size("node")
    n_z = Z_SIZE
    n_x = n_batch // n_z
    _, slots, feature_dim = cotangent.shape
    table_rows = embed_table.shape[0]
    width = feature_dim // n_node
    half = width // 2
    heads = width // HEAD_DIM
    entries = n_batch * PAIR_ROWS
    vmem = pl.BlockSpec(memory_space=pltpu.VMEM)
    smem = pl.BlockSpec(memory_space=pltpu.SMEM)
    anywhere = pl.BlockSpec(memory_space=pl.ANY)
    shaped = jax.ShapeDtypeStruct
    dma = pltpu.SemaphoreType.DMA

    rows, reqs, dest = pl.pallas_call(
        functools.partial(fetch_kernel, n_batch, n_node),
        out_shape=(
            shaped((n_node, slots, width), BF16),
            shaped((2, n_batch, 1, 128), I32),
            shaped((1, slots), I32),
        ),
        in_specs=[vmem, vmem, anywhere],
        out_specs=(vmem, vmem, vmem),
        scratch_shapes=[
            pltpu.VMEM((table_rows, width), BF16),
            pltpu.VMEM((n_batch, 1, 128), I32),
            pltpu.VMEM((entries, 128), I32),
            pltpu.VMEM((n_batch, PAIR_ROWS, width), BF16),
            pltpu.VMEM((n_batch, PAIR_ROWS, width), BF16),
            dma,
            dma((4,)),
            dma((4,)),
        ],
        compiler_params=pltpu.CompilerParams(
            collective_id=0, has_side_effects=True, vmem_limit_bytes=24 * 2**20
        ),
        name="fetch_rows",
    )(owner_shard.reshape(1, slots), local_row.reshape(1, slots), embed_table)

    grads, d_rows, small = pl.pallas_call(
        layer_kernel,
        out_shape=(
            shaped((4, 2, 4, feature_dim // 8, width), BF16),
            shaped((n_node, slots, width), BF16),
            shaped((8, heads * (NSPD + NDEG)), F32),
        ),
        in_specs=[smem, smem, smem] + [vmem] * 8,
        out_specs=(vmem, vmem, vmem),
        scratch_shapes=[
            pltpu.VMEM((heads, slots, slots), F32),
            pltpu.VMEM((heads, slots, slots), F32),
            pltpu.VMEM((heads * (NSPD + NDEG), 128), F32),
        ],
        compiler_params=pltpu.CompilerParams(vmem_limit_bytes=48 * 2**20),
        name="layer",
    )(
        lengths,
        spd_bias,
        degree_bias,
        rows,
        spd_bucket.reshape(slots, slots),
        degree_bucket,
        cotangent.reshape(slots, feature_dim),
        w_query,
        w_key,
        w_value,
        w_out,
    )

    chunks = 4
    quarter = feature_dim // 8
    piece = quarter // n_z
    small_shape = small.shape
    out, table_grad, small = pl.pallas_call(
        functools.partial(reduce_kernel, n_batch, n_node),
        out_shape=(
            shaped((chunks, 2, n_x, n_z, piece, width), BF16),
            shaped((table_rows, half), F32),
            shaped(small_shape, F32),
        ),
        in_specs=[vmem] * 5,
        out_specs=(vmem, vmem, vmem),
        scratch_shapes=[
            pltpu.VMEM((chunks, n_x, quarter, width), BF16),
            pltpu.VMEM((chunks, n_x, quarter, width), BF16),
            pltpu.VMEM((chunks, n_x, quarter, width), BF16),
            pltpu.VMEM((chunks, n_z, piece, width), BF16),
            pltpu.VMEM((chunks, n_z, piece, width), BF16),
            pltpu.VMEM((n_node, slots, width), BF16),
            pltpu.VMEM((2, n_batch, PAIR_ROWS, half), BF16),
            pltpu.VMEM((n_batch, PAIR_ROWS, half), BF16),
            pltpu.VMEM((2, n_batch, PAIR_ROWS, half), BF16),
            pltpu.VMEM(small_shape, F32),
            pltpu.VMEM((n_x,) + small_shape, F32),
            pltpu.VMEM((n_z,) + small_shape, F32),
            pltpu.VMEM((entries, 128), I32),
            dma((6, chunks)),
            dma((6, chunks)),
            dma((3,)),
            dma((3,)),
            dma((3,)),
            dma((3,)),
        ],
        compiler_params=pltpu.CompilerParams(
            collective_id=1, has_side_effects=True, vmem_limit_bytes=48 * 2**20
        ),
        name="reduce_gradients",
    )(grads, d_rows, small, dest, reqs)

    out = out.reshape(chunks, feature_dim, width).astype(F32)
    by_bucket = small[0].reshape(heads, NSPD + NDEG).T
    out_grad = out[0].reshape(n_node, width, width).transpose(1, 0, 2).reshape(width, feature_dim)
    return (
        table_grad,
        out[3],
        out[2],
        out[1],
        out_grad,
        by_bucket[:NSPD],
        by_bucket[NSPD:],
    )


def solution(mesh):
    placed = (
        P("batch", None),
        P(("batch", "replica"), None, None),
        P(("batch", "replica"), None),
        P(("batch", "replica")),
        P(("batch", "replica"), None, None),
        P(("batch", "replica"), None),
        P(None, "node"),
        P(None, "node"),
        P(None, "node"),
        P("node", None),
        P(None, "node"),
        P(None, "node"),
        P(("batch", "replica"), None, None),
    )
    return jax.shard_map(
        on_device,
        mesh=mesh,
        in_specs=placed,
        out_specs=(
            P("batch", ("node", "replica")),
            P(None, "node"),
            P(None, "node"),
            P(None, "node"),
            P("node", None),
            P(None, "node"),
            P(None, "node"),
        ),
        check_vma=False,
    )
```

time: 311 us -> 104 us (0.33)
  blocking collectives: 185 us -> 0 us
  Pallas kernels: 0 us -> 91.7 us
  other arithmetic: 29.4 us -> 0 us
  matrix products: 26.8 us -> 0 us
  waiting for transfers between devices: 25.7 us -> 0 us
  between operations: 16.5 us -> 1.38 us
  local copies, waits for them, and re-layouts: 21.6 us -> 10.9 us
  starting transfers between devices: 4.93 us -> 0 us
    psum x1 -> x0, blocking collectives: 127 us -> none  [on_device(): lax.psum((query_part, key_part, value_part, out_part, spd_part, degree_pa...]
    pallas_call x0 -> x3, Pallas kernels: none -> 91.7 us  [the longest x1 52.5 us: on_device(): pl.pallas_call(functools.partial(reduce_kernel, n_batch, n_node), out_sha...]
    all_to_all x2 -> x0, blocking collectives: 57.1 us -> none  [the longest x1 36.8 us: on_device(): lax.all_to_all(send_back.reshape(peer_count, capacity, feature_dim).astyp...]
    dot_general x21 -> x0, matrix products: 26.8 us -> none  [the longest x1 3.96 us: on_device(): jnp.einsum('gijb,ghij->bh', spd_hot, d_scores, precision=lax.Precision.HI...]
    all_to_all x1 -> x0, waiting for transfers between devices: 18.4 us -> none  [on_device(): lax.all_to_all(embed_table[safe_rows].reshape(peer_count, capacity, featu...]
    convert_element_type x4 -> x0, other arithmetic: 7.99 us -> none  [the longest x1 3.91 us: on_device(): accum.astype(jnp.bfloat16)]
    psum x1 -> x0, waiting for transfers between devices: 7.24 us -> none  [on_device(): lax.psum((query_part, key_part, value_part, out_part, spd_part, degree_pa...]
    scatter-add x1 -> x0, other arithmetic: 6.66 us -> none  [on_device(): jnp.zeros((row_count, feature_dim), jnp.float32).at[target_rows]]
  transfers between devices with their start and end apart: 3 -> 0, of which waited for: 2 -> 0; matrix products, arithmetic and copies ran while one was open for 14% -> 0% of each run, Pallas kernels for 0% -> 0%
where the time goes in v1:
time: 104 us
  Pallas kernels  91.7 us (88%)
  local copies, waits for them, and re-layouts  10.9 us (10%)
  between operations  1.38 us (1%)
    pallas_call x1, Pallas kernels, on_device(): pl.pallas_call(functools.partial(reduce_kernel, n_batch, n_node), out_sha...  52.5 us
    pallas_call x1, Pallas kernels, on_device(): pl.pallas_call(functools.partial(fetch_kernel, n_batch, n_node), out_shap...  29.8 us
    pallas_call x1, Pallas kernels, on_device(): pl.pallas_call(layer_kernel, out_shape=(shaped((4, 2, 4, feature_dim // 8...  9.33 us
    unnamed x25, local copies, waits for them, and re-layouts  7.27 us

profile of v1, /device:TPU:1, one launch (start us, length us, event | category | flops | bytes accessed | tf_op | source)
XLA Modules:
  0.0 104.0 jit_solution(13877291016710647813)
XLA Ops:
  0.6 0.0 copy-start.9
  1.3 0.8 copy.20.spd_bias_ref
  2.1 0.8 copy.21.deg_bias_ref
  2.8 0.0 copy-start
  2.8 1.6 %copy-done = bf16[1024,1024]{1,0:T(8,128)(2,1)S(1)} copy-done((bf16[1024,1024]{1,0:T(8,128)(2,1)S(1)}, bf16[1024,1024]{1,0:T(8,128)(2,1)}, u32[]{:S(2)}) %copy-start) | copy-done | bytes 2097176
  4.4 0.0 copy-start.7
  4.4 0.7 copy-done.7
  5.1 0.0 copy-start.8
  5.1 0.7 copy-done.8
  5.8 0.0 copy-start.1
  5.8 0.0 copy-start.2
  5.8 0.0 copy-start.3
  5.8 0.0 copy-start.4
  5.8 29.8 %fetch_rows.1 = (bf16[4,256,256]{2,1,0:T(8,128)(2,1)S(1)}, s32[2,32,1,128]{3,2,1,0:T(1,128)S(1)}, s32[1,256]{1,0:T(1,128)S(1)}) custom-call(s32[1,256]{1,0:T(1,128)S(1)} %bitcast.15, s32[1,256]{1,0:T(1,128)S(1)} %copy-done.8, bf16[1024,1024]{1,0:T(8,128)(2,1)S(1)} %copy-done), custom_call_target="tpu_custom_call" | custom-call | tf_op jit(solution)/shard_map/fetch_rows/pallas_call | solution.py:540
  35.6 0.0 copy-done.9
  35.7 0.0 copy-done.1
  35.7 0.0 copy-done.2
  35.7 0.0 copy-done.3
  35.7 0.0 copy-done.4
  35.7 0.0 copy-start.5
  35.7 1.0 copy-done.5
  36.7 0.0 copy-start.6
  36.7 0.9 copy-done.6
  37.7 9.3 %layer.1 = (bf16[4,2,4,128,256]{4,3,2,1,0:T(8,128)(2,1)S(1)}, bf16[4,256,256]{2,1,0:T(8,128)(2,1)S(1)}, f32[8,192]{1,0:T(8,128)S(1)}) custom-call(s32[1]{0:T(128)S(6)} %copy.25.length_ref, f32[16,4]{1,0:T(8,128)S(1)} %copy.20.spd_bias_ref, f32[32,4]{1,0:T(8,128)S(1)} %copy.21.deg_bias_ref, bf16[4,256,256]{2,1,0:T(8,128)(2,1)S(1)} %get-tuple-element.16.rows_ref, ...), custom_call_target="tpu_custom_call" | custom-call | tf_op jit(solution)/shard_map/layer/pallas_call | solution.py:565
  47.0 52.5 %reduce_gradients.1 = (bf16[4,2,4,8,16,256]{5,4,3,2,1,0:T(8,128)(2,1)S(1)}, f32[1024,128]{1,0:T(8,128)S(1)}, f32[8,192]{1,0:T(8,128)S(1)}) custom-call(bf16[4,2,4,128,256]{4,3,2,1,0:T(8,128)(2,1)S(1)} %get-tuple-element.17.grads_ref, bf16[4,256,256]{2,1,0:T(8,128)(2,1)S(1)} %get-tuple-element.18.d_rows_ref, f32[8,192]{1,0:T(8,128)S(1)} %get-tuple-element.19.small_ref, ...), custom_call_target="tpu_custom_call" | custom-call | tf_op jit(solution)/shard_map/reduce_gradients/pallas_call | solution.py:599
  99.5 0.1 reshape_squeeze.7
  99.6 0.0 copy-start.10
  99.6 0.7 slice.31
  100.3 1.8 %fusion = (f32[1,2,4,8,16,256]{5,4,3,2,1,0:T(8,128)S(1)}, f32[1,2,4,8,16,256]{5,4,3,2,1,0:T(8,128)}, f32[1,2,4,8,16,256]{5,4,3,2,1,0:T(8,128)}, f32[1,2,4,8,16,256]{5,4,3,2,1,0:T(8,128)}) fusion(bf16[4,2,4,8,16,256]{5,4,3,2,1,0:T(8,128)(2,1)S(1)} %get-tuple-element.23), kind=kLoop, calls=%fused_computation.1 | loop fusion | bytes 8388608 | tf_op jit(solution)/shard_map/slice | solution.py:637
  102.1 0.0 copy-done.10
  102.1 1.1 %copy.23 = f32[4,32,8,256]{3,2,0,1:T(8,128)} copy(f32[4,32,8,256]{3,2,1,0:T(8,128)S(1)} %bitcast.16) | data formatting | bytes 2097152 | tf_op jit(solution)/shard_map/reshape | solution.py:637
  103.2 0.8 copy.26
  (1 shorter events, 0.0 us)
Async XLA Ops:
  0.6 35.0 %copy-start.9 = (s32[1,256]{1,0:T(1,128)S(1)}, s32[1,256]{1,0:T(1,128)}, u32[]{:S(2)}) copy-start(s32[1,256]{1,0:T(1,128)} %deg_ref.1) | copy-start | bytes 3076
  2.8 1.6 %copy-start = (bf16[1024,1024]{1,0:T(8,128)(2,1)S(1)}, bf16[1024,1024]{1,0:T(8,128)(2,1)}, u32[]{:S(2)}) copy-start(bf16[1024,1024]{1,0:T(8,128)(2,1)} %table_ref.1) | copy-start | bytes 6291460
  4.4 0.7 copy-start.7
  5.1 0.7 copy-start.8
  5.8 29.9 %copy-start.1 = (bf16[1,256,1024]{2,1,0:T(8,128)(2,1)S(1)}, bf16[1,256,1024]{2,1,0:T(8,128)(2,1)}, u32[]{:S(2)}) copy-start(bf16[1,256,1024]{2,1,0:T(8,128)(2,1)} %param.25) | copy-start | bytes 1572868
  5.8 29.9 %copy-start.2 = (bf16[1024,256]{1,0:T(8,128)(2,1)S(1)}, bf16[1024,256]{1,0:T(8,128)(2,1)}, u32[]{:S(2)}) copy-start(bf16[1024,256]{1,0:T(8,128)(2,1)} %wq_ref.1) | copy-start | bytes 1572868
  5.8 29.9 %copy-start.3 = (bf16[1024,256]{1,0:T(8,128)(2,1)S(1)}, bf16[1024,256]{1,0:T(8,128)(2,1)}, u32[]{:S(2)}) copy-start(bf16[1024,256]{1,0:T(8,128)(2,1)} %wk_ref.1) | copy-start | bytes 1572868
  5.8 29.9 %copy-start.4 = (bf16[1024,256]{1,0:T(8,128)(2,1)S(1)}, bf16[1024,256]{1,0:T(8,128)(2,1)}, u32[]{:S(2)}) copy-start(bf16[1024,256]{1,0:T(8,128)(2,1)} %wv_ref.1) | copy-start | bytes 1572868
  35.7 1.0 %copy-start.5 = (bf16[256,1024]{1,0:T(8,128)(2,1)S(1)}, bf16[256,1024]{1,0:T(8,128)(2,1)}, u32[]{:S(2)}) copy-start(bf16[256,1024]{1,0:T(8,128)(2,1)} %wo_ref.1) | copy-start | bytes 1572868
  36.7 0.9 copy-start.6
  99.6 2.5 %copy-start.10 = (f32[4,48]{1,0:T(4,128)}, f32[4,48]{1,0:T(4,128)S(1)}, u32[]{:S(2)}) copy-start(f32[4,48]{1,0:T(4,128)S(1)} %reshape_squeeze.7) | copy-start | bytes 2308

commit v2 on v0

v2 whole, which is shorter than its diff:
```python
import functools

import jax
import jax.numpy as jnp
from jax import lax
from jax.experimental import pallas as pl
from jax.experimental.pallas import tpu as pltpu
from jax.sharding import PartitionSpec as P

HEAD_DIM = 64
NSPD = 16
NDEG = 32
EPS = 1e-05
PAIR_ROWS = 16
Z_SIZE = 8
MESH = pl.DeviceIdType.MESH
F32 = jnp.float32
BF16 = jnp.bfloat16
I32 = jnp.int32


def iota(shape, dim):
    return lax.broadcasted_iota(I32, shape, dim)


def dot(a, b, ca=1, cb=0, precision=None):
    return lax.dot_general(
        a, b, (((ca,), (cb,)), ((), ())), preferred_element_type=F32, precision=precision
    )


def remote(src, dst, send_sem, recv_sem, **where):
    return pltpu.make_async_remote_copy(
        src_ref=src,
        dst_ref=dst,
        send_sem=send_sem,
        recv_sem=recv_sem,
        device_id=where,
        device_id_type=MESH,
    )


def wait_bytes(ref, sem):
    pltpu.make_async_copy(ref, ref, sem).wait()


def train_kernel(
    n_batch,
    n_node,
    length_ref,
    spd_bias_ref,
    deg_bias_ref,
    owner_hbm,
    local_hbm,
    deg_hbm,
    table_hbm,
    spd_hbm,
    cot_hbm,
    wo_hbm,
    wq_hbm,
    wk_hbm,
    wv_hbm,
    out_hbm,
    table_hbm_out,
    small_hbm,
    owner_v,
    local_v,
    deg_v,
    table_v,
    spd_v,
    cot_v,
    wo_v,
    wq_v,
    wk_v,
    wv_v,
    ask,
    reqs,
    spread,
    rows_send,
    rows_recv,
    rows,
    dest_v,
    bias,
    d_att_v,
    probs_v,
    d_scores,
    sums,
    small,
    grads,
    d_rows_v,
    core_in,
    core_sum,
    x1_in,
    x2_in,
    x_sum,
    z_in,
    y_in,
    pack,
    to_core,
    table_in,
    small_core,
    small_x,
    small_z,
    out_ref,
    table_ref,
    small_out,
    lsem,
    gs,
    gr,
    ssem,
    rsem,
    fs,
    fr,
    ts,
    tr,
    wsem,
):
    me_b, me_n, me_r = lax.axis_index("batch"), lax.axis_index("node"), lax.axis_index("replica")
    n_z = Z_SIZE
    n_x = n_batch // n_z
    me_x, me_z = me_b // n_z, me_b % n_z
    other = 1 - me_r
    up, down, across_x = lax.rem(me_x + 1, n_x), lax.rem(me_x + 3, n_x), lax.rem(me_x + 2, n_x)
    slots, feature_dim = cot_v.shape
    table_rows, width = table_v.shape
    heads = width // HEAD_DIM
    blocks = feature_dim // width
    half = width // 2
    entries = n_batch * PAIR_ROWS
    chunks = out_ref.shape[0]
    piece = out_ref.shape[4]
    quarter = n_z * piece
    copies = 2.0 * n_batch
    scale = HEAD_DIM ** (-0.5)
    step = 32
    z_order = (4, 3, 5, 2, 6, 1, 7)
    barrier = pltpu.get_barrier_semaphore()

    def signal_batch(j, carry):
        p = lax.rem(me_b + j, n_batch)
        pl.semaphore_signal(barrier, inc=1, device_id={"batch": p}, device_id_type=MESH)
        return carry

    lax.fori_loop(1, n_batch, signal_batch, 0)
    for j in range(1, n_node):
        p = lax.rem(me_n + j, n_node)
        pl.semaphore_signal(barrier, inc=1, device_id={"node": p}, device_id_type=MESH)
    pl.semaphore_signal(barrier, inc=1, device_id={"replica": other}, device_id_type=MESH)

    columns = pl.ds(pl.multiple_of(me_n * width, width), width)
    loads = [
        pltpu.make_async_copy(src, dst, lsem.at[i])
        for i, (src, dst) in enumerate(
            (
                (owner_hbm, owner_v),
                (local_hbm, local_v),
                (deg_hbm, deg_v),
                (spd_hbm, spd_v),
                (table_hbm.at[:, columns], table_v),
                (cot_hbm, cot_v),
                (wo_hbm, wo_v),
                (wq_hbm, wq_v),
                (wk_hbm, wk_v),
                (wv_hbm, wv_v),
            )
        )
    ]
    for load in loads:
        load.start()

    loads[0].wait()
    loads[1].wait()
    owner_row = owner_v[...]
    across = jnp.broadcast_to(owner_row, (slots, slots))
    owner_down = jnp.transpose(across)
    same = across == owner_down
    r0, r1 = iota((slots, slots), 0), iota((slots, slots), 1)
    rank_row = jnp.sum(jnp.where(same & (r0 < r1), 1.0, 0.0), axis=0, keepdims=True).astype(I32)
    rank_col = jnp.sum(jnp.where(same & (r1 < r0), 1.0, 0.0), axis=1, keepdims=True).astype(I32)
    dest_v[...] = owner_row * PAIR_ROWS + rank_row
    dest_col = owner_down[:, 0:1] * PAIR_ROWS + rank_col

    wanted = local_v[...] + 1
    hit = owner_row == iota((n_batch, slots), 0)
    high = jnp.where(hit, (wanted // 32).astype(F32), 0.0).astype(BF16)
    low = jnp.where(hit, (wanted % 32).astype(F32), 0.0).astype(BF16)
    at_rank = jnp.where(rank_col == iota((slots, 128), 1), 1.0, 0.0).astype(BF16)
    listed = (dot(high, at_rank) * 32.0 + dot(low, at_rank)).astype(I32)
    for o in range(n_batch):
        ask[o] = listed[o : o + 1, :]

    pl.semaphore_wait(barrier, n_batch - 1 + n_node - 1 + 1)

    def send_ask(j, carry):
        p = lax.rem(me_b + j, n_batch)
        remote(ask.at[p], reqs.at[me_r, me_b], gs.at[0], gr.at[0], batch=p).start()
        return carry

    lax.fori_loop(1, n_batch, send_ask, 0)
    reqs[me_r, me_b] = ask[me_b]

    loads[2].wait()
    loads[3].wait()

    def bias_block(i, carry):
        at = pl.ds(pl.multiple_of(i * step, step), step)
        bucket = spd_v[at, :]
        terms = [jnp.full(bucket.shape, spd_bias_ref[h, 0], F32) for h in range(heads)]
        for b in range(1, NSPD):
            is_b = bucket == b
            terms = [jnp.where(is_b, spd_bias_ref[h, b], terms[h]) for h in range(heads)]
        for h in range(heads):
            bias[h, at, :] = terms[h]
        return carry

    lax.fori_loop(0, slots // step, bias_block, 0)
    place = jnp.where(iota((slots, entries), 1) == dest_col, 1.0, 0.0).astype(BF16)

    loads[4].wait()
    wait_bytes(ask.at[pl.ds(0, n_batch - 1)], gr.at[0])
    remote(reqs.at[me_r], reqs.at[me_r], gs.at[1], gr.at[1], replica=other).start()
    group = n_z * PAIR_ROWS
    mine = iota((group, 128), 1) == iota((group, 128), 0) % PAIR_ROWS
    for dx in (2, 1, 3, 0):
        first = lax.rem(me_x + dx, n_x) * n_z
        for k in range(n_z):
            spread[k * PAIR_ROWS : (k + 1) * PAIR_ROWS, :] = jnp.broadcast_to(
                reqs[me_r, first + k], (PAIR_ROWS, 128)
            )
        listed = spread[0:group, :].astype(F32)
        target = jnp.sum(jnp.where(mine, listed, 0.0), axis=1, keepdims=True).astype(I32) - 1
        pick = jnp.where(iota((group, table_rows), 1) == target, 1.0, 0.0).astype(BF16)
        rows_send[pl.ds(first, n_z)] = (
            dot(pick, table_v[...]).astype(BF16).reshape(n_z, PAIR_ROWS, width)
        )
        for dz in z_order + ((0,) if dx else ()):
            p = first + lax.rem(me_z + dz, n_z)
            remote(rows_send.at[p], rows_recv.at[me_b], gs.at[2], gr.at[2], batch=p).start()
    rows_recv[me_b] = rows_send[me_b]

    loads[5].wait()
    loads[6].wait()
    length = length_ref[0]
    d_masked = jnp.where(
        iota((slots, feature_dim), 0) < length, cot_v[...].astype(F32), 0.0
    ).astype(BF16)
    cot_v[...] = d_masked
    d_att_v[...] = dot(d_masked, wo_v[...], 1, 1).astype(BF16)
    degree = deg_v[...]
    deg_terms = []
    for h in range(heads):
        term = jnp.full(degree.shape, deg_bias_ref[h, 0], F32)
        for b in range(1, NDEG):
            term = jnp.where(degree == b, deg_bias_ref[h, b], term)
        deg_terms.append(term)

    wait_bytes(rows_recv.at[pl.ds(0, n_batch - 1)], gr.at[2])
    rows[me_n] = dot(place, rows_recv[...].reshape(entries, width)).astype(BF16)
    for j in (2, 1, 3):
        p = lax.rem(me_n + j, n_node)
        remote(rows.at[me_n], rows.at[me_n], gs.at[3], gr.at[3], node=p).start()
    for load in loads[7:]:
        load.wait()
    wait_bytes(rows.at[pl.ds(0, n_node - 1)], gr.at[3])

    def core_send(c):
        remote(grads.at[c, other], core_in.at[c], ssem.at[0, c], rsem.at[0, c], replica=other).start()

    def x_far(c):
        wait_bytes(core_in.at[c], rsem.at[0, c])
        core_sum[c] = (grads[c, me_r].astype(F32) + core_in[c].astype(F32)).astype(BF16)
        for d, to in enumerate((up, down)):
            remote(
                core_sum.at[c, across_x, pl.ds(d * (quarter // 2), quarter // 2)],
                x1_in.at[c, d],
                ssem.at[1, c],
                rsem.at[1, c],
                batch=to * n_z + me_z,
            ).start()

    def x_near(c):
        wait_bytes(x1_in.at[c], rsem.at[1, c])
        for d, to in enumerate((up, down)):
            part = pl.ds(d * (quarter // 2), quarter // 2)
            core_sum[c, to, part] = (
                core_sum[c, to, part].astype(F32) + x1_in[c, d].astype(F32)
            ).astype(BF16)
            remote(
                core_sum.at[c, to],
                x2_in.at[c, d],
                ssem.at[2, c],
                rsem.at[2, c],
                batch=to * n_z + me_z,
            ).start()

    def z_send(c):
        wait_bytes(x2_in.at[c], rsem.at[2, c])
        total = core_sum[c, me_x].astype(F32) + x2_in[c, 0].astype(F32) + x2_in[c, 1].astype(F32)
        x_sum[c] = total.astype(BF16).reshape(n_z, piece, width)
        for j in z_order:
            p = lax.rem(me_z + j, n_z)
            remote(
                x_sum.at[c, p],
                z_in.at[c, me_z],
                ssem.at[3, c],
                rsem.at[3, c],
                batch=me_x * n_z + p,
            ).start()
        z_in[c, me_z] = x_sum[c, me_z]

    def z_back(c):
        wait_bytes(z_in.at[c, pl.ds(0, n_z - 1)], rsem.at[3, c])
        total = z_in[c, 0].astype(F32)
        for z in range(1, n_z):
            total = total + z_in[c, z].astype(F32)
        out_ref[c, me_r, me_x, me_z] = (total * (1.0 / copies)).astype(BF16)
        done = out_ref.at[c, me_r, me_x, me_z]
        for j in z_order:
            p = lax.rem(me_z + j, n_z)
            remote(done, done, ssem.at[4, c], rsem.at[4, c], batch=me_x * n_z + p).start()

    def x_back(c):
        wait_bytes(out_ref.at[c, 0, 0, pl.ds(0, n_z - 1)], rsem.at[4, c])
        done = out_ref.at[c, me_r, me_x]
        for to in (up, down):
            remote(done, done, ssem.at[5, c], rsem.at[5, c], batch=to * n_z + me_z).start()

    def x_pass(c):
        wait_bytes(out_ref.at[c, 0, pl.ds(0, 2)], rsem.at[5, c])
        for d, (source, to) in enumerate(((down, up), (up, down))):
            done = out_ref.at[c, me_r, source, pl.ds(d * (n_z // 2), n_z // 2)]
            remote(done, done, ssem.at[6, c], rsem.at[6, c], batch=to * n_z + me_z).start()

    def core_back(c):
        wait_bytes(out_ref.at[c, 0, 0], rsem.at[6, c])
        done = out_ref.at[c, me_r]
        remote(done, done, ssem.at[7, c], rsem.at[7, c], replica=other).start()

    x = jnp.concatenate([rows[b] for b in range(blocks)], axis=1).astype(F32)
    centred = x - jnp.mean(x, axis=1, keepdims=True)
    inv_std = lax.rsqrt(jnp.mean(centred * centred, axis=1, keepdims=True) + EPS)
    x_hat = centred * inv_std
    normed = x_hat.astype(BF16)
    queries = dot(normed, wq_v[...]).astype(BF16)
    keys = dot(normed, wk_v[...]).astype(BF16)
    values = dot(normed, wv_v[...]).astype(BF16)
    normed_t = jnp.transpose(normed)
    d_att = d_att_v[...]

    lane_head = iota((slots, width), 1) // HEAD_DIM

    def only(h, a):
        return jnp.where(lane_head == h, a, jnp.zeros_like(a))

    valid = iota((slots, slots), 1) < length
    attended = jnp.zeros((slots, width), F32)
    d_values = jnp.zeros((slots, width), F32)
    for h in range(heads):
        scores = dot(only(h, queries), keys, 1, 1) * scale + bias[h] + deg_terms[h]
        scores = jnp.where(valid, scores, -jnp.inf)
        exps = jnp.exp(scores - jnp.max(scores, axis=1, keepdims=True))
        probs = exps / jnp.sum(exps, axis=1, keepdims=True)
        probs_v[h] = probs
        probs_b = probs.astype(BF16)
        attended = attended + dot(probs_b, only(h, values))
        d_values = d_values + dot(probs_b, only(h, d_att), 0, 0)
    out_part = dot(attended.astype(BF16), cot_v[...], 0, 0).astype(BF16)
    for b in range(blocks):
        for k in range(2):
            grads[0, b // 2, 2 * (b % 2) + k] = out_part[
                k * quarter : (k + 1) * quarter, b * width : (b + 1) * width
            ]
    core_send(0)
    halves = (2, n_x, quarter, width)
    d_values = d_values.astype(BF16)
    grads[1] = dot(normed_t, d_values).astype(BF16).reshape(halves)
    core_send(1)

    d_queries = jnp.zeros((slots, width), F32)
    d_keys = jnp.zeros((slots, width), F32)
    for h in range(heads):
        probs = probs_v[h]
        d_probs = dot(only(h, d_att), values, 1, 1)
        ds = probs * (d_probs - jnp.sum(probs * d_probs, axis=1, keepdims=True))
        d_scores[h] = ds
        ds_b = ds.astype(BF16)
        d_queries = d_queries + dot(ds_b, only(h, keys))
        d_keys = d_keys + dot(ds_b, only(h, queries), 0, 0)
    d_queries = (d_queries * scale).astype(BF16)
    d_keys = (d_keys * scale).astype(BF16)
    x_far(0)
    grads[2] = dot(normed_t, d_keys).astype(BF16).reshape(halves)
    core_send(2)
    x_far(1)
    grads[3] = dot(normed_t, d_queries).astype(BF16).reshape(halves)
    core_send(3)
    x_near(0)

    d_normed = (
        dot(d_queries, wq_v[...], 1, 1)
        + dot(d_keys, wk_v[...], 1, 1)
        + dot(d_values, wv_v[...], 1, 1)
    )
    lead = jnp.where(me_n == 0, 1.0, 0.0)
    d_rows = lead * cot_v[...].astype(F32) + inv_std * (
        d_normed
        - jnp.mean(d_normed, axis=1, keepdims=True)
        - x_hat * jnp.mean(d_normed * x_hat, axis=1, keepdims=True)
    )
    for b in range(blocks):
        d_rows_v[b] = d_rows[:, b * width : (b + 1) * width].astype(BF16)
    for j in (2, 1, 3):
        p = lax.rem(me_n + j, n_node)
        remote(d_rows_v.at[p], y_in.at[me_n], fs.at[0], fr.at[0], node=p).start()
    y_in[me_n] = d_rows_v[me_n]

    def bucket_sums(h):
        def spd_block(i, totals):
            at = pl.ds(pl.multiple_of(i * step, step), step)
            bucket, ds = spd_v[at, :], d_scores[h, at, :]
            new = []
            for b in range(NSPD):
                kept = jnp.where(bucket == b, ds, 0.0)
                kept = kept[:, :128] + kept[:, 128:]
                new.append(totals[b] + (kept[0:8] + kept[8:16]) + (kept[16:24] + kept[24:32]))
            return tuple(new)

        totals = lax.fori_loop(
            0, slots // step, spd_block, tuple(jnp.zeros((8, 128), F32) for _ in range(NSPD))
        )
        sums[h * 128 : (h + 1) * 128, :] = jnp.zeros((128, 128), F32)
        for b in range(NSPD):
            at = h * 128 + b
            sums[at : at + 1, :] = jnp.sum(totals[b], axis=0, keepdims=True)
        by_key = jnp.sum(d_scores[h], axis=0, keepdims=True)
        kept = jnp.where(degree == iota((NDEG, slots), 0), by_key, 0.0)
        at = h * 128 + NSPD
        sums[at : at + NDEG, :] = kept[:, :128] + kept[:, 128:]

    x_far(2)
    x_near(1)
    x_far(3)
    z_send(0)
    bucket_sums(0)
    x_near(2)
    z_send(1)
    bucket_sums(1)
    x_near(3)

    lists = jnp.where(iota((entries, slots), 0) == dest_v[...], 1.0, 0.0).astype(BF16)
    wait_bytes(y_in.at[pl.ds(0, n_node - 1)], fr.at[0])
    d_rows = y_in[0].astype(F32)
    for n in range(1, n_node):
        d_rows = d_rows + y_in[n].astype(F32)
    packed = dot(lists, d_rows.astype(BF16)).astype(BF16)
    left, right = packed[:, :half], packed[:, half:]
    shape = (n_batch, PAIR_ROWS, half)
    to_core[...] = jnp.where(me_r == 0, right, left).reshape(shape)
    remote(to_core, pack.at[me_r], fs.at[1], fr.at[1], replica=other).start()
    pack[me_r] = jnp.where(me_r == 0, left, right).reshape(shape)

    z_send(2)
    z_back(0)
    bucket_sums(2)
    wait_bytes(to_core, fr.at[1])
    for dx in (2, 1, 3, 0):
        first = lax.rem(me_x + dx, n_x) * n_z
        for dz in z_order + ((0,) if dx else ()):
            p = first + lax.rem(me_z + dz, n_z)
            remote(pack.at[:, p], table_in.at[:, me_b], fs.at[2], fr.at[2], batch=p).start()
    table_in[:, me_b] = pack[:, me_b]
    z_send(3)
    z_back(1)
    bucket_sums(3)
    totals = dot(jnp.ones((8, 128), F32), sums[...], 1, 1, precision=lax.Precision.HIGHEST)
    small[...] = jnp.zeros_like(small)
    for h in range(heads):
        small[h : h + 1, :] = totals[0:1, h * 128 : (h + 1) * 128]
    remote(small, small_core, ts.at[0], tr.at[0], replica=other).start()
    z_back(2)
    x_back(0)
    wait_bytes(small_core, tr.at[0])
    small_x[me_x] = small[...] + small_core[...]
    for j in (2, 1, 3):
        p = lax.rem(me_x + j, n_x)
        remote(
            small_x.at[me_x], small_x.at[me_x], ts.at[1], tr.at[1], batch=p * n_z + me_z
        ).start()
    z_back(3)
    x_back(1)

    wait_bytes(reqs.at[0], gr.at[1])
    mine = iota((entries, 128), 1) == iota((entries, 128), 0) % PAIR_ROWS
    targets = []
    for r in range(2):
        for p in range(n_batch):
            spread[p * PAIR_ROWS : (p + 1) * PAIR_ROWS, :] = jnp.broadcast_to(
                reqs[r, p], (PAIR_ROWS, 128)
            )
        target = jnp.sum(jnp.where(mine, spread[...].astype(F32), 0.0), axis=1, keepdims=True) - 1.0
        flat = jnp.transpose(jnp.broadcast_to(target, (entries, 128)))[0:1, :].astype(I32)
        targets.append(flat)
    x_pass(0)
    x_back(2)
    wait_bytes(small_x.at[pl.ds(0, n_x - 1)], tr.at[1])
    total = small_x[0]
    for x in range(1, n_x):
        total = total + small_x[x]
    small_z[me_z] = total
    for j in z_order:
        p = lax.rem(me_z + j, n_z)
        remote(
            small_z.at[me_z], small_z.at[me_z], ts.at[2], tr.at[2], batch=me_x * n_z + p
        ).start()
    x_pass(1)
    x_back(3)
    core_back(0)

    row = iota((table_rows, entries), 0)
    scatter = [jnp.where(row == t, 1.0, 0.0).astype(BF16) for t in targets]
    wait_bytes(table_in.at[:, pl.ds(0, n_batch - 1)], fr.at[2])
    table_ref[...] = dot(scatter[0], table_in[0].reshape(entries, half)) + dot(
        scatter[1], table_in[1].reshape(entries, half)
    )
    writes = [pltpu.make_async_copy(table_ref, table_hbm_out, wsem.at[chunks])]
    writes[0].start()
    x_pass(2)
    core_back(1)
    x_pass(3)
    core_back(2)
    wait_bytes(small_z.at[pl.ds(0, n_z - 1)], tr.at[2])
    total = small_z[0]
    for z in range(1, n_z):
        total = total + small_z[z]
    small_out[...] = total * (1.0 / copies)
    core_back(3)
    writes.append(pltpu.make_async_copy(small_out, small_hbm, wsem.at[chunks + 1]))
    writes[-1].start()
    for c in range(chunks):
        wait_bytes(out_ref.at[c, 0], rsem.at[7, c])
        writes.append(pltpu.make_async_copy(out_ref.at[c], out_hbm.at[c], wsem.at[c]))
        writes[-1].start()

    wait_bytes(ask.at[pl.ds(0, n_batch - 1)], gs.at[0])
    wait_bytes(reqs.at[0], gs.at[1])
    wait_bytes(rows_send.at[pl.ds(0, n_batch - 1)], gs.at[2])
    wait_bytes(rows.at[pl.ds(0, n_node - 1)], gs.at[3])
    wait_bytes(y_in.at[pl.ds(0, n_node - 1)], fs.at[0])
    wait_bytes(to_core, fs.at[1])
    wait_bytes(table_in.at[:, pl.ds(0, n_batch - 1)], fs.at[2])
    wait_bytes(small_core, ts.at[0])
    wait_bytes(small_x.at[pl.ds(0, n_x - 1)], ts.at[1])
    wait_bytes(small_z.at[pl.ds(0, n_z - 1)], ts.at[2])
    for c in range(chunks):
        wait_bytes(core_in.at[c], ssem.at[0, c])
        wait_bytes(x1_in.at[c], ssem.at[1, c])
        wait_bytes(x2_in.at[c], ssem.at[2, c])
        wait_bytes(z_in.at[c, pl.ds(0, n_z - 1)], ssem.at[3, c])
        wait_bytes(out_ref.at[c, 0, 0, pl.ds(0, n_z - 1)], ssem.at[4, c])
        wait_bytes(out_ref.at[c, 0, pl.ds(0, 2)], ssem.at[5, c])
        wait_bytes(out_ref.at[c, 0, 0], ssem.at[6, c])
        wait_bytes(out_ref.at[c, 0], ssem.at[7, c])
    for write in writes:
        write.wait()


def finish_kernel(
    sums_hbm,
    table_hbm,
    small_hbm,
    table_out,
    query_out,
    key_out,
    value_out,
    out_out,
    spd_out,
    deg_out,
    sums_v,
    small_v,
    table_v,
    wide,
    outer,
    rsem,
    wsem,
):
    chunks = sums_v.shape[0]
    width = outer.shape[0]
    reads = [
        pltpu.make_async_copy(sums_hbm.at[c], sums_v.at[c], rsem.at[c]) for c in range(chunks)
    ]
    reads.append(pltpu.make_async_copy(small_hbm, small_v, rsem.at[chunks]))
    reads.append(pltpu.make_async_copy(table_hbm, table_v, rsem.at[chunks + 1]))
    for read in reads:
        read.start()
    reads[0].wait()
    step = 64
    steps = width // step

    def widen_outer(i, carry):
        at = pl.ds(pl.multiple_of(i * step, step), step)
        for b in range(outer.shape[1] // width):
            row = pl.ds(pl.multiple_of(i * step + b * width, step), step)
            outer[at, b * width : (b + 1) * width] = sums_v[0, row].astype(F32)
        return carry

    lax.fori_loop(0, steps, widen_outer, 0)
    writes = [pltpu.make_async_copy(outer, out_out, wsem.at[0])]
    writes[0].start()
    for c, out in ((1, value_out), (2, key_out), (3, query_out)):
        reads[c].wait()

        def widen(i, carry, c=c):
            at = pl.ds(pl.multiple_of(i * width, width), width)
            wide[c - 1, at] = sums_v[c, at].astype(F32)
            return carry

        lax.fori_loop(0, sums_v.shape[1] // width, widen, 0)
        writes.append(pltpu.make_async_copy(wide.at[c - 1], out, wsem.at[c]))
        writes[-1].start()
    reads[chunks + 1].wait()
    writes.append(pltpu.make_async_copy(table_v, table_out, wsem.at[chunks]))
    writes[-1].start()
    reads[chunks].wait()
    heads = spd_out.shape[0]
    spd_out[...] = small_v[0:heads, 0:NSPD]
    deg_out[...] = small_v[0:heads, NSPD : NSPD + NDEG]
    for write in writes:
        write.wait()


def on_device(
    embed_table,
    owner_shard,
    local_row,
    lengths,
    spd_bucket,
    degree_bucket,
    w_query,
    w_key,
    w_value,
    w_out,
    spd_bias,
    degree_bias,
    cotangent,
):
    n_batch, n_node = lax.axis_size("batch"), lax.axis_size("node")
    n_z = Z_SIZE
    n_x = n_batch // n_z
    _, slots, feature_dim = cotangent.shape
    table_rows = embed_table.shape[0]
    width = feature_dim // n_node
    half = width // 2
    heads = width // HEAD_DIM
    entries = n_batch * PAIR_ROWS
    chunks = 4
    quarter = feature_dim // (2 * n_x)
    piece = quarter // n_z
    vmem = pl.BlockSpec(memory_space=pltpu.VMEM)
    smem = pl.BlockSpec(memory_space=pltpu.SMEM)
    hbm = pl.BlockSpec(memory_space=pltpu.HBM)
    shaped = jax.ShapeDtypeStruct
    dma = pltpu.SemaphoreType.DMA
    v = pltpu.VMEM

    sums, table_grad, small = pl.pallas_call(
        functools.partial(train_kernel, n_batch, n_node),
        out_shape=(
            shaped((chunks, 2, n_x, n_z, piece, width), BF16),
            shaped((table_rows, half), F32),
            shaped((8, 128), F32),
        ),
        in_specs=[smem] * 3 + [hbm] * 10,
        out_specs=(hbm, hbm, hbm),
        scratch_shapes=[
            v((1, slots), I32),
            v((1, slots), I32),
            v((1, slots), I32),
            v((table_rows, width), BF16),
            v((slots, slots), I32),
            v((slots, feature_dim), BF16),
            v((width, feature_dim), BF16),
            v((feature_dim, width), BF16),
            v((feature_dim, width), BF16),
            v((feature_dim, width), BF16),
            v((n_batch, 1, 128), I32),
            v((2, n_batch, 1, 128), I32),
            v((entries, 128), I32),
            v((n_batch, PAIR_ROWS, width), BF16),
            v((n_batch, PAIR_ROWS, width), BF16),
            v((n_node, slots, width), BF16),
            v((1, slots), I32),
            v((heads, slots, slots), F32),
            v((slots, width), BF16),
            v((heads, slots, slots), F32),
            v((heads, slots, slots), F32),
            v((heads * 128, 128), F32),
            v((8, 128), F32),
            v((chunks, 2, n_x, quarter, width), BF16),
            v((n_node, slots, width), BF16),
            v((chunks, n_x, quarter, width), BF16),
            v((chunks, n_x, quarter, width), BF16),
            v((chunks, 2, quarter // 2, width), BF16),
            v((chunks, 2, quarter, width), BF16),
            v((chunks, n_z, piece, width), BF16),
            v((chunks, n_z, piece, width), BF16),
            v((n_node, slots, width), BF16),
            v((2, n_batch, PAIR_ROWS, half), BF16),
            v((n_batch, PAIR_ROWS, half), BF16),
            v((2, n_batch, PAIR_ROWS, half), BF16),
            v((8, 128), F32),
            v((n_x, 8, 128), F32),
            v((n_z, 8, 128), F32),
            v((chunks, 2, n_x, n_z, piece, width), BF16),
            v((table_rows, half), F32),
            v((8, 128), F32),
            dma((10,)),
            dma((4,)),
            dma((4,)),
            dma((8, chunks)),
            dma((8, chunks)),
            dma((3,)),
            dma((3,)),
            dma((3,)),
            dma((3,)),
            dma((chunks + 2,)),
        ],
        compiler_params=pltpu.CompilerParams(
            collective_id=0, has_side_effects=True, vmem_limit_bytes=61 * 2**20
        ),
        name="layer_and_exchanges",
    )(
        lengths,
        spd_bias.T,
        degree_bias.T,
        owner_shard.reshape(1, slots),
        local_row,
        degree_bucket,
        embed_table,
        spd_bucket.reshape(slots, slots),
        cotangent.reshape(slots, feature_dim),
        w_out,
        w_query,
        w_key,
        w_value,
    )

    square = shaped((feature_dim, width), F32)
    table_grad, query_grad, key_grad, value_grad, out_grad, spd_grad, degree_grad = pl.pallas_call(
        finish_kernel,
        out_shape=(
            shaped((table_rows, half), F32),
            square,
            square,
            square,
            shaped((width, feature_dim), F32),
            shaped((heads, NSPD), F32),
            shaped((heads, NDEG), F32),
        ),
        in_specs=[hbm] * 3,
        out_specs=(hbm,) * 5 + (vmem, vmem),
        scratch_shapes=[
            v((chunks, feature_dim, width), BF16),
            v((8, 128), F32),
            v((table_rows, half), F32),
            v((3, feature_dim, width), F32),
            v((width, feature_dim), F32),
            dma((chunks + 2,)),
            dma((chunks + 1,)),
        ],
        compiler_params=pltpu.CompilerParams(vmem_limit_bytes=61 * 2**20),
        name="write_outputs",
    )(sums.reshape(chunks, feature_dim, width), table_grad, small)
    return table_grad, query_grad, key_grad, value_grad, out_grad, spd_grad.T, degree_grad.T


def solution(mesh):
    placed = (
        P("batch", None),
        P(("batch", "replica"), None, None),
        P(("batch", "replica"), None),
        P(("batch", "replica")),
        P(("batch", "replica"), None, None),
        P(("batch", "replica"), None),
        P(None, "node"),
        P(None, "node"),
        P(None, "node"),
        P("node", None),
        P(None, "node"),
        P(None, "node"),
        P(("batch", "replica"), None, None),
    )
    return jax.shard_map(
        on_device,
        mesh=mesh,
        in_specs=placed,
        out_specs=(
            P("batch", ("node", "replica")),
            P(None, "node"),
            P(None, "node"),
            P(None, "node"),
            P("node", None),
            P(None, "node"),
            P(None, "node"),
        ),
        check_vma=False,
    )
```

time: 311 us -> 83.6 us (0.27)
  blocking collectives: 185 us -> 0 us
  Pallas kernels: 0 us -> 82.2 us
  other arithmetic: 29.4 us -> 0 us
  matrix products: 26.8 us -> 0 us
  waiting for transfers between devices: 25.7 us -> 0 us
  local copies, waits for them, and re-layouts: 21.6 us -> 0 us
  between operations: 16.5 us -> 1.29 us
  starting transfers between devices: 4.93 us -> 0 us
    psum x1 -> x0, blocking collectives: 127 us -> none  [on_device(): lax.psum((query_part, key_part, value_part, out_part, spd_part, degree_pa...]
    pallas_call x0 -> x2, Pallas kernels: none -> 82.2 us  [the longest x1 78.2 us: on_device(): pl.pallas_call(functools.partial(train_kernel, n_batch, n_node), out_shap...]
    all_to_all x2 -> x0, blocking collectives: 57.1 us -> none  [the longest x1 36.8 us: on_device(): lax.all_to_all(send_back.reshape(peer_count, capacity, feature_dim).astyp...]
    dot_general x21 -> x0, matrix products: 26.8 us -> none  [the longest x1 3.96 us: on_device(): jnp.einsum('gijb,ghij->bh', spd_hot, d_scores, precision=lax.Precision.HI...]
    all_to_all x1 -> x0, waiting for transfers between devices: 18.4 us -> none  [on_device(): lax.all_to_all(embed_table[safe_rows].reshape(peer_count, capacity, featu...]
    convert_element_type x4 -> x0, other arithmetic: 7.99 us -> none  [the longest x1 3.91 us: on_device(): accum.astype(jnp.bfloat16)]
    psum x1 -> x0, waiting for transfers between devices: 7.24 us -> none  [on_device(): lax.psum((query_part, key_part, value_part, out_part, spd_part, degree_pa...]
    unnamed x42 -> x0, local copies, waits for them, and re-layouts: 7.14 us -> none
  transfers between devices with their start and end apart: 3 -> 0, of which waited for: 2 -> 0; matrix products, arithmetic and copies ran while one was open for 14% -> 0% of each run, Pallas kernels for 0% -> 0%
where the time goes in v2:
time: 83.6 us; the launch traced here: 83.5 us
  Pallas kernels  82.2 us (98%)
  between operations  1.29 us (2%)
    pallas_call x1, Pallas kernels, on_device(): pl.pallas_call(functools.partial(train_kernel, n_batch, n_node), out_shap...  78.2 us
    pallas_call x1, Pallas kernels, on_device(): pl.pallas_call(finish_kernel, out_shape=(shaped((table_rows, half), F32),...  3.97 us

profile of v2, /device:TPU:1, one launch (start us, length us, event | category | flops | bytes accessed | tf_op | source)
XLA Modules:
  0.0 83.5 jit_solution(15216714687296087563)
XLA Ops:
  1.3 78.2 %layer_and_exchanges.1 = (bf16[4,2,4,8,16,256]{5,4,3,2,1,0:T(8,128)(2,1)}, f32[1024,128]{1,0:T(8,128)}, f32[8,128]{1,0:T(8,128)}) custom-call(s32[1]{0:T(128)S(6)} %copy.20.length_ref, f32[4,16]{1,0:T(4,128)} %bitcast.11, f32[4,32]{1,0:T(4,128)} %bitcast.12, s32[1,256]{1,0:T(1,128)} %bitcast.13, s32[1,256]{1,0:T(1,128)} %local_hbm.1, s32[1,256]{1,0:T(1,128)} %deg_hbm.1, ...), custom_call_target="tpu_custom_call" | custom-call | tf_op jit(solution)/shard_map/layer_and_exchanges/pallas_call | solution.py:665
  79.5 4.0 %write_outputs.1 = (f32[1024,128]{1,0:T(8,128)}, f32[1024,256]{1,0:T(8,128)}, f32[1024,256]{1,0:T(8,128)}, f32[1024,256]{1,0:T(8,128)}, f32[256,1024]{1,0:T(8,128)}, /*index=5*/f32[4,16]{1,0:T(4,128)}, f32[4,32]{1,0:T(4,128)}) custom-call(bf16[4,1024,256]{2,1,0:T(8,128)(2,1)} %bitcast.8, f32[1024,128]{1,0:T(8,128)} %get-tuple-element.18.table_hbm, ...), custom_call_target="tpu_custom_call" | custom-call | tf_op jit(solution)/shard_map/write_outputs/pallas_call | solution.py:748

commit v3 on v2

--- a/solution.py
+++ b/solution.py
@@ -47,9 +47,9 @@
 def train_kernel(
     n_batch,
     n_node,
-    length_ref,
     spd_bias_ref,
     deg_bias_ref,
+    length_hbm,
     owner_hbm,
     local_hbm,
     deg_hbm,
@@ -63,6 +63,7 @@
     out_hbm,
     table_hbm_out,
     small_hbm,
+    length_ref,
     owner_v,
     local_v,
     deg_v,
@@ -90,8 +91,8 @@
     d_rows_v,
     core_in,
     core_sum,
-    x1_in,
-    x2_in,
+    x_far_in,
+    x_in,
     x_sum,
     z_in,
     y_in,
@@ -101,6 +102,7 @@
     small_core,
     small_x,
     small_z,
+    scatter,
     out_ref,
     table_ref,
     small_out,
@@ -109,6 +111,7 @@
     gr,
     ssem,
     rsem,
+    xsem,
     fs,
     fr,
     ts,
@@ -162,6 +165,7 @@
                 (wq_hbm, wq_v),
                 (wk_hbm, wk_v),
                 (wv_hbm, wv_v),
+                (length_hbm, length_ref),
             )
         )
     ]
@@ -240,7 +244,8 @@
 
     loads[5].wait()
     loads[6].wait()
-    length = length_ref[0]
+    loads[10].wait()
+    length = length_ref[...]
     d_masked = jnp.where(
         iota((slots, feature_dim), 0) < length, cot_v[...].astype(F32), 0.0
     ).astype(BF16)
@@ -259,57 +264,65 @@
     for j in (2, 1, 3):
         p = lax.rem(me_n + j, n_node)
         remote(rows.at[me_n], rows.at[me_n], gs.at[3], gr.at[3], node=p).start()
-    for load in loads[7:]:
+    for load in loads[7:10]:
         load.wait()
     wait_bytes(rows.at[pl.ds(0, n_node - 1)], gr.at[3])
 
     def core_send(c):
         remote(grads.at[c, other], core_in.at[c], ssem.at[0, c], rsem.at[0, c], replica=other).start()
+
+    first_half, last_half = pl.ds(0, quarter // 2), pl.ds(quarter // 2, quarter // 2)
 
     def x_far(c):
         wait_bytes(core_in.at[c], rsem.at[0, c])
         core_sum[c] = (grads[c, me_r].astype(F32) + core_in[c].astype(F32)).astype(BF16)
-        for d, to in enumerate((up, down)):
+        for d, (to, part) in enumerate(((up, first_half), (down, last_half))):
             remote(
-                core_sum.at[c, across_x, pl.ds(d * (quarter // 2), quarter // 2)],
-                x1_in.at[c, d],
+                core_sum.at[c, across_x, part],
+                x_far_in.at[c, d],
                 ssem.at[1, c],
                 rsem.at[1, c],
                 batch=to * n_z + me_z,
             ).start()
 
+    def x_share(c, d, to, part):
+        remote(
+            core_sum.at[c, to, part],
+            x_in.at[c, d, part],
+            ssem.at[6, c],
+            rsem.at[6, c],
+            batch=to * n_z + me_z,
+        ).start()
+
+    def x_own(c):
+        x_share(c, 0, up, last_half)
+        x_share(c, 1, down, first_half)
+
     def x_near(c):
-        wait_bytes(x1_in.at[c], rsem.at[1, c])
-        for d, to in enumerate((up, down)):
-            part = pl.ds(d * (quarter // 2), quarter // 2)
+        wait_bytes(x_far_in.at[c], rsem.at[1, c])
+        for d, (to, part) in enumerate(((up, first_half), (down, last_half))):
             core_sum[c, to, part] = (
-                core_sum[c, to, part].astype(F32) + x1_in[c, d].astype(F32)
+                core_sum[c, to, part].astype(F32) + x_far_in[c, d].astype(F32)
             ).astype(BF16)
-            remote(
-                core_sum.at[c, to],
-                x2_in.at[c, d],
-                ssem.at[2, c],
-                rsem.at[2, c],
-                batch=to * n_z + me_z,
-            ).start()
+            x_share(c, d, to, part)
 
     def z_send(c):
-        wait_bytes(x2_in.at[c], rsem.at[2, c])
-        total = core_sum[c, me_x].astype(F32) + x2_in[c, 0].astype(F32) + x2_in[c, 1].astype(F32)
+        wait_bytes(x_in.at[c], rsem.at[6, c])
+        total = core_sum[c, me_x].astype(F32) + x_in[c, 0].astype(F32) + x_in[c, 1].astype(F32)
         x_sum[c] = total.astype(BF16).reshape(n_z, piece, width)
         for j in z_order:
             p = lax.rem(me_z + j, n_z)
             remote(
                 x_sum.at[c, p],
                 z_in.at[c, me_z],
-                ssem.at[3, c],
-                rsem.at[3, c],
+                ssem.at[2, c],
+                rsem.at[2, c],
                 batch=me_x * n_z + p,
             ).start()
         z_in[c, me_z] = x_sum[c, me_z]
 
     def z_back(c):
-        wait_bytes(z_in.at[c, pl.ds(0, n_z - 1)], rsem.at[3, c])
+        wait_bytes(z_in.at[c, pl.ds(0, n_z - 1)], rsem.at[2, c])
         total = z_in[c, 0].astype(F32)
         for z in range(1, n_z):
             total = total + z_in[c, z].astype(F32)
@@ -317,24 +330,40 @@
         done = out_ref.at[c, me_r, me_x, me_z]
         for j in z_order:
             p = lax.rem(me_z + j, n_z)
-            remote(done, done, ssem.at[4, c], rsem.at[4, c], batch=me_x * n_z + p).start()
+            remote(done, done, ssem.at[3, c], rsem.at[3, c], batch=me_x * n_z + p).start()
+
+    def core_back(c, x):
+        done = out_ref.at[c, me_r, x]
+        remote(done, done, ssem.at[5, c], rsem.at[5, c], replica=other).start()
+
+    low, high = pl.ds(0, n_z // 2), pl.ds(n_z // 2, n_z // 2)
+
+    def x_give(c, k, source, part, to):
+        done = out_ref.at[c, me_r, source, part]
+        remote(done, done, ssem.at[4, c], xsem.at[k, c], batch=to * n_z + me_z).start()
 
     def x_back(c):
-        wait_bytes(out_ref.at[c, 0, 0, pl.ds(0, n_z - 1)], rsem.at[4, c])
-        done = out_ref.at[c, me_r, me_x]
-        for to in (up, down):
-            remote(done, done, ssem.at[5, c], rsem.at[5, c], batch=to * n_z + me_z).start()
+        wait_bytes(out_ref.at[c, 0, 0, pl.ds(0, n_z - 1)], rsem.at[3, c])
+        x_give(c, 0, me_x, low, up)
+        x_give(c, 1, me_x, high, down)
+        x_give(c, 2, me_x, high, up)
+        x_give(c, 3, me_x, low, down)
 
     def x_pass(c):
-        wait_bytes(out_ref.at[c, 0, pl.ds(0, 2)], rsem.at[5, c])
-        for d, (source, to) in enumerate(((down, up), (up, down))):
-            done = out_ref.at[c, me_r, source, pl.ds(d * (n_z // 2), n_z // 2)]
-            remote(done, done, ssem.at[6, c], rsem.at[6, c], batch=to * n_z + me_z).start()
-
-    def core_back(c):
-        wait_bytes(out_ref.at[c, 0, 0], rsem.at[6, c])
-        done = out_ref.at[c, me_r]
-        remote(done, done, ssem.at[7, c], rsem.at[7, c], replica=other).start()
+        wait_bytes(out_ref.at[c, 0, 0, low], xsem.at[0, c])
+        x_give(c, 4, down, low, up)
+        wait_bytes(out_ref.at[c, 0, 0, low], xsem.at[1, c])
+        x_give(c, 4, up, high, down)
+
+    def x_done(c):
+        wait_bytes(out_ref.at[c, 0, 0, low], xsem.at[2, c])
+        core_back(c, down)
+        wait_bytes(out_ref.at[c, 0, 0, low], xsem.at[3, c])
+        core_back(c, up)
+
+    def x_last(c):
+        wait_bytes(out_ref.at[c, 0, 0], xsem.at[4, c])
+        core_back(c, across_x)
 
     x = jnp.concatenate([rows[b] for b in range(blocks)], axis=1).astype(F32)
     centred = x - jnp.mean(x, axis=1, keepdims=True)
@@ -389,12 +418,11 @@
     d_queries = (d_queries * scale).astype(BF16)
     d_keys = (d_keys * scale).astype(BF16)
     x_far(0)
+    x_far(1)
     grads[2] = dot(normed_t, d_keys).astype(BF16).reshape(halves)
     core_send(2)
-    x_far(1)
     grads[3] = dot(normed_t, d_queries).astype(BF16).reshape(halves)
     core_send(3)
-    x_near(0)
 
     d_normed = (
         dot(d_queries, wq_v[...], 1, 1)
@@ -438,14 +466,15 @@
         sums[at : at + NDEG, :] = kept[:, :128] + kept[:, 128:]
 
     x_far(2)
-    x_near(1)
     x_far(3)
-    z_send(0)
+    for c in range(chunks):
+        x_own(c)
     bucket_sums(0)
-    x_near(2)
-    z_send(1)
+    for c in range(chunks):
+        x_near(c)
     bucket_sums(1)
-    x_near(3)
+    for c in range(chunks):
+        z_send(c)
 
     lists = jnp.where(iota((entries, slots), 0) == dest_v[...], 1.0, 0.0).astype(BF16)
     wait_bytes(y_in.at[pl.ds(0, n_node - 1)], fr.at[0])
@@ -459,17 +488,8 @@
     remote(to_core, pack.at[me_r], fs.at[1], fr.at[1], replica=other).start()
     pack[me_r] = jnp.where(me_r == 0, left, right).reshape(shape)
 
-    z_send(2)
+    bucket_sums(2)
     z_back(0)
-    bucket_sums(2)
-    wait_bytes(to_core, fr.at[1])
-    for dx in (2, 1, 3, 0):
-        first = lax.rem(me_x + dx, n_x) * n_z
-        for dz in z_order + ((0,) if dx else ()):
-            p = first + lax.rem(me_z + dz, n_z)
-            remote(pack.at[:, p], table_in.at[:, me_b], fs.at[2], fr.at[2], batch=p).start()
-    table_in[:, me_b] = pack[:, me_b]
-    z_send(3)
     z_back(1)
     bucket_sums(3)
     totals = dot(jnp.ones((8, 128), F32), sums[...], 1, 1, precision=lax.Precision.HIGHEST)
@@ -478,16 +498,14 @@
         small[h : h + 1, :] = totals[0:1, h * 128 : (h + 1) * 128]
     remote(small, small_core, ts.at[0], tr.at[0], replica=other).start()
     z_back(2)
-    x_back(0)
-    wait_bytes(small_core, tr.at[0])
-    small_x[me_x] = small[...] + small_core[...]
-    for j in (2, 1, 3):
-        p = lax.rem(me_x + j, n_x)
-        remote(
-            small_x.at[me_x], small_x.at[me_x], ts.at[1], tr.at[1], batch=p * n_z + me_z
-        ).start()
     z_back(3)
-    x_back(1)
+    wait_bytes(to_core, fr.at[1])
+    for dx in (2, 1, 3, 0):
+        first = lax.rem(me_x + dx, n_x) * n_z
+        for dz in z_order + ((0,) if dx else ()):
+            p = first + lax.rem(me_z + dz, n_z)
+            remote(pack.at[:, p], table_in.at[:, me_b], fs.at[2], fr.at[2], batch=p).start()
+    table_in[:, me_b] = pack[:, me_b]
 
     wait_bytes(reqs.at[0], gr.at[1])
     mine = iota((entries, 128), 1) == iota((entries, 128), 0) % PAIR_ROWS
@@ -500,8 +518,22 @@
         target = jnp.sum(jnp.where(mine, spread[...].astype(F32), 0.0), axis=1, keepdims=True) - 1.0
         flat = jnp.transpose(jnp.broadcast_to(target, (entries, 128)))[0:1, :].astype(I32)
         targets.append(flat)
-    x_pass(0)
-    x_back(2)
+    wait_bytes(small_core, tr.at[0])
+    small_x[me_x] = small[...] + small_core[...]
+    for to in (across_x, up, down):
+        remote(
+            small_x.at[me_x], small_x.at[me_x], ts.at[1], tr.at[1], batch=to * n_z + me_z
+        ).start()
+
+    for c in range(chunks):
+        x_back(c)
+    for c in range(chunks):
+        core_back(c, me_x)
+    row = iota((table_rows, entries), 0)
+    for r in range(2):
+        scatter[r] = jnp.where(row == targets[r], 1.0, 0.0).astype(BF16)
+    for c in range(chunks):
+        x_pass(c)
     wait_bytes(small_x.at[pl.ds(0, n_x - 1)], tr.at[1])
     total = small_x[0]
     for x in range(1, n_x):
@@ -512,32 +544,26 @@
         remote(
             small_z.at[me_z], small_z.at[me_z], ts.at[2], tr.at[2], batch=me_x * n_z + p
         ).start()
-    x_pass(1)
-    x_back(3)
-    core_back(0)
-
-    row = iota((table_rows, entries), 0)
-    scatter = [jnp.where(row == t, 1.0, 0.0).astype(BF16) for t in targets]
+
+    for c in range(chunks):
+        x_done(c)
     wait_bytes(table_in.at[:, pl.ds(0, n_batch - 1)], fr.at[2])
     table_ref[...] = dot(scatter[0], table_in[0].reshape(entries, half)) + dot(
         scatter[1], table_in[1].reshape(entries, half)
     )
     writes = [pltpu.make_async_copy(table_ref, table_hbm_out, wsem.at[chunks])]
     writes[0].start()
-    x_pass(2)
-    core_back(1)
-    x_pass(3)
-    core_back(2)
+    for c in range(chunks):
+        x_last(c)
     wait_bytes(small_z.at[pl.ds(0, n_z - 1)], tr.at[2])
     total = small_z[0]
     for z in range(1, n_z):
         total = total + small_z[z]
     small_out[...] = total * (1.0 / copies)
-    core_back(3)
     writes.append(pltpu.make_async_copy(small_out, small_hbm, wsem.at[chunks + 1]))
     writes[-1].start()
     for c in range(chunks):
-        wait_bytes(out_ref.at[c, 0], rsem.at[7, c])
+        wait_bytes(out_ref.at[c, 0], rsem.at[5, c])
         writes.append(pltpu.make_async_copy(out_ref.at[c], out_hbm.at[c], wsem.at[c]))
         writes[-1].start()
 
@@ -553,13 +579,12 @@
     wait_bytes(small_z.at[pl.ds(0, n_z - 1)], ts.at[2])
     for c in range(chunks):
         wait_bytes(core_in.at[c], ssem.at[0, c])
-        wait_bytes(x1_in.at[c], ssem.at[1, c])
-        wait_bytes(x2_in.at[c], ssem.at[2, c])
-        wait_bytes(z_in.at[c, pl.ds(0, n_z - 1)], ssem.at[3, c])
-        wait_bytes(out_ref.at[c, 0, 0, pl.ds(0, n_z - 1)], ssem.at[4, c])
-        wait_bytes(out_ref.at[c, 0, pl.ds(0, 2)], ssem.at[5, c])
-        wait_bytes(out_ref.at[c, 0, 0], ssem.at[6, c])
-        wait_bytes(out_ref.at[c, 0], ssem.at[7, c])
+        wait_bytes(x_far_in.at[c], ssem.at[1, c])
+        wait_bytes(x_in.at[c], ssem.at[6, c])
+        wait_bytes(z_in.at[c, pl.ds(0, n_z - 1)], ssem.at[2, c])
+        wait_bytes(out_ref.at[c, 0, 0, pl.ds(0, n_z - 1)], ssem.at[3, c])
+        wait_bytes(out_ref.at[c, 0, pl.ds(0, n_x - 1)], ssem.at[4, c])
+        wait_bytes(out_ref.at[c, 0], ssem.at[5, c])
     for write in writes:
         write.wait()
 
@@ -669,9 +694,10 @@
             shaped((table_rows, half), F32),
             shaped((8, 128), F32),
         ),
-        in_specs=[smem] * 3 + [hbm] * 10,
+        in_specs=[smem] * 2 + [hbm] * 11,
         out_specs=(hbm, hbm, hbm),
         scratch_shapes=[
+            v((1, 1), I32),
             v((1, slots), I32),
             v((1, slots), I32),
             v((1, slots), I32),
@@ -710,14 +736,16 @@
             v((8, 128), F32),
             v((n_x, 8, 128), F32),
             v((n_z, 8, 128), F32),
+            v((2, table_rows, entries), BF16),
             v((chunks, 2, n_x, n_z, piece, width), BF16),
             v((table_rows, half), F32),
             v((8, 128), F32),
-            dma((10,)),
+            dma((11,)),
             dma((4,)),
             dma((4,)),
-            dma((8, chunks)),
-            dma((8, chunks)),
+            dma((7, chunks)),
+            dma((7, chunks)),
+            dma((5, chunks)),
             dma((3,)),
             dma((3,)),
             dma((3,)),
@@ -729,9 +757,9 @@
         ),
         name="layer_and_exchanges",
     )(
-        lengths,
         spd_bias.T,
         degree_bias.T,
+        lengths.reshape(1, 1),
         owner_shard.reshape(1, slots),
         local_row,
         degree_bucket,

time: 83.6 us -> 78 us (0.933)
  Pallas kernels: 82.2 us -> 76.5 us
    pallas_call x1, Pallas kernels: 78.2 us -> 72.5 us  [on_device(): pl.pallas_call(functools.partial(train_kernel, n_batch, n_node), out_shap...]
where the time goes in v3:
time: 78 us; the launch traced here: 77.8 us
  Pallas kernels  76.5 us (98%)
  between operations  1.29 us (2%)
    pallas_call x1, Pallas kernels, on_device(): pl.pallas_call(functools.partial(train_kernel, n_batch, n_node), out_shap...  72.5 us
    pallas_call x1, Pallas kernels, on_device(): pl.pallas_call(finish_kernel, out_shape=(shaped((table_rows, half), F32),...  3.97 us

profile of v3, /device:TPU:1, one launch (start us, length us, event | category | flops | bytes accessed | tf_op | source)
XLA Modules:
  0.0 77.8 jit_solution(2087370991803058577)
XLA Ops:
  1.3 72.5 %layer_and_exchanges.1 = (bf16[4,2,4,8,16,256]{5,4,3,2,1,0:T(8,128)(2,1)}, f32[1024,128]{1,0:T(8,128)}, f32[8,128]{1,0:T(8,128)}) custom-call(f32[4,16]{1,0:T(4,128)} %bitcast.13, f32[4,32]{1,0:T(4,128)} %bitcast.14, s32[1,1]{1,0:T(1,128)} %bitcast.9.length_hbm, s32[1,256]{1,0:T(1,128)} %bitcast.15, s32[1,256]{1,0:T(1,128)} %local_hbm.1, s32[1,256]{1,0:T(1,128)} %deg_hbm.1, ...), custom_call_target="tpu_custom_call" | custom-call | tf_op jit(solution)/shard_map/layer_and_exchanges/pallas_call | solution.py:690
  73.8 4.0 %write_outputs.1 = (f32[1024,128]{1,0:T(8,128)}, f32[1024,256]{1,0:T(8,128)}, f32[1024,256]{1,0:T(8,128)}, f32[1024,256]{1,0:T(8,128)}, f32[256,1024]{1,0:T(8,128)}, /*index=5*/f32[4,16]{1,0:T(4,128)}, f32[4,32]{1,0:T(4,128)}) custom-call(bf16[4,1024,256]{2,1,0:T(8,128)(2,1)} %bitcast.10, f32[1024,128]{1,0:T(8,128)} %get-tuple-element.18.table_hbm, ...), custom_call_target="tpu_custom_call" | custom-call | tf_op jit(solution)/shard_map/write_outputs/pallas_call | solution.py:776

commit v4 on v3

--- a/solution.py
+++ b/solution.py
@@ -103,6 +103,7 @@
     small_x,
     small_z,
     scatter,
+    lists,
     out_ref,
     table_ref,
     small_out,
@@ -264,6 +265,21 @@
     for j in (2, 1, 3):
         p = lax.rem(me_n + j, n_node)
         remote(rows.at[me_n], rows.at[me_n], gs.at[3], gr.at[3], node=p).start()
+    wait_bytes(reqs.at[0], gr.at[1])
+    mine = iota((entries, 128), 1) == iota((entries, 128), 0) % PAIR_ROWS
+    targets = []
+    for r in range(2):
+        for p in range(n_batch):
+            spread[p * PAIR_ROWS : (p + 1) * PAIR_ROWS, :] = jnp.broadcast_to(
+                reqs[r, p], (PAIR_ROWS, 128)
+            )
+        target = jnp.sum(jnp.where(mine, spread[...].astype(F32), 0.0), axis=1, keepdims=True) - 1.0
+        flat = jnp.transpose(jnp.broadcast_to(target, (entries, 128)))[0:1, :].astype(I32)
+        targets.append(flat)
+    row = iota((table_rows, entries), 0)
+    for r in range(2):
+        scatter[r] = jnp.where(row == targets[r], 1.0, 0.0).astype(BF16)
+    lists[...] = jnp.where(iota((entries, slots), 0) == dest_v[...], 1.0, 0.0).astype(BF16)
     for load in loads[7:10]:
         load.wait()
     wait_bytes(rows.at[pl.ds(0, n_node - 1)], gr.at[3])
@@ -272,6 +288,8 @@
         remote(grads.at[c, other], core_in.at[c], ssem.at[0, c], rsem.at[0, c], replica=other).start()
 
     first_half, last_half = pl.ds(0, quarter // 2), pl.ds(quarter // 2, quarter // 2)
+
+    straight = (0, 1)
 
     def x_far(c):
         wait_bytes(core_in.at[c], rsem.at[0, c])
@@ -282,7 +300,7 @@
                 x_far_in.at[c, d],
                 ssem.at[1, c],
                 rsem.at[1, c],
-                batch=to * n_z + me_z,
+                batch=(across_x if c in straight else to) * n_z + me_z,
             ).start()
 
     def x_share(c, d, to, part):
@@ -297,8 +315,13 @@
     def x_own(c):
         x_share(c, 0, up, last_half)
         x_share(c, 1, down, first_half)
+        if c in straight:
+            x_share(c, 0, up, first_half)
+            x_share(c, 1, down, last_half)
 
     def x_near(c):
+        if c in straight:
+            return
         wait_bytes(x_far_in.at[c], rsem.at[1, c])
         for d, (to, part) in enumerate(((up, first_half), (down, last_half))):
             core_sum[c, to, part] = (
@@ -309,6 +332,9 @@
     def z_send(c):
         wait_bytes(x_in.at[c], rsem.at[6, c])
         total = core_sum[c, me_x].astype(F32) + x_in[c, 0].astype(F32) + x_in[c, 1].astype(F32)
+        if c in straight:
+            wait_bytes(x_far_in.at[c], rsem.at[1, c])
+            total = total + x_far_in[c].astype(F32).reshape(quarter, width)
         x_sum[c] = total.astype(BF16).reshape(n_z, piece, width)
         for j in z_order:
             p = lax.rem(me_z + j, n_z)
@@ -476,12 +502,11 @@
     for c in range(chunks):
         z_send(c)
 
-    lists = jnp.where(iota((entries, slots), 0) == dest_v[...], 1.0, 0.0).astype(BF16)
     wait_bytes(y_in.at[pl.ds(0, n_node - 1)], fr.at[0])
     d_rows = y_in[0].astype(F32)
     for n in range(1, n_node):
         d_rows = d_rows + y_in[n].astype(F32)
-    packed = dot(lists, d_rows.astype(BF16)).astype(BF16)
+    packed = dot(lists[...], d_rows.astype(BF16)).astype(BF16)
     left, right = packed[:, :half], packed[:, half:]
     shape = (n_batch, PAIR_ROWS, half)
     to_core[...] = jnp.where(me_r == 0, right, left).reshape(shape)
@@ -507,17 +532,6 @@
             remote(pack.at[:, p], table_in.at[:, me_b], fs.at[2], fr.at[2], batch=p).start()
     table_in[:, me_b] = pack[:, me_b]
 
-    wait_bytes(reqs.at[0], gr.at[1])
-    mine = iota((entries, 128), 1) == iota((entries, 128), 0) % PAIR_ROWS
-    targets = []
-    for r in range(2):
-        for p in range(n_batch):
-            spread[p * PAIR_ROWS : (p + 1) * PAIR_ROWS, :] = jnp.broadcast_to(
-                reqs[r, p], (PAIR_ROWS, 128)
-            )
-        target = jnp.sum(jnp.where(mine, spread[...].astype(F32), 0.0), axis=1, keepdims=True) - 1.0
-        flat = jnp.transpose(jnp.broadcast_to(target, (entries, 128)))[0:1, :].astype(I32)
-        targets.append(flat)
     wait_bytes(small_core, tr.at[0])
     small_x[me_x] = small[...] + small_core[...]
     for to in (across_x, up, down):
@@ -529,9 +543,6 @@
         x_back(c)
     for c in range(chunks):
         core_back(c, me_x)
-    row = iota((table_rows, entries), 0)
-    for r in range(2):
-        scatter[r] = jnp.where(row == targets[r], 1.0, 0.0).astype(BF16)
     for c in range(chunks):
         x_pass(c)
     wait_bytes(small_x.at[pl.ds(0, n_x - 1)], tr.at[1])
@@ -737,6 +748,7 @@
             v((n_x, 8, 128), F32),
             v((n_z, 8, 128), F32),
             v((2, table_rows, entries), BF16),
+            v((entries, slots), BF16),
             v((chunks, 2, n_x, n_z, piece, width), BF16),
             v((table_rows, half), F32),
             v((8, 128), F32),

time: 78 us -> 77.7 us (level)
  no operation moved by 1% of the time
where the time goes in v4:
time: 77.7 us; the launch traced here: 77.5 us
  Pallas kernels  76.2 us (98%)
  between operations  1.29 us (2%)
    pallas_call x1, Pallas kernels, on_device(): pl.pallas_call(functools.partial(train_kernel, n_batch, n_node), out_shap...  72.3 us
    pallas_call x1, Pallas kernels, on_device(): pl.pallas_call(finish_kernel, out_shape=(shaped((table_rows, half), F32),...  3.97 us

profile of v4, /device:TPU:1, one launch (start us, length us, event | category | flops | bytes accessed | tf_op | source)
XLA Modules:
  0.0 77.5 jit_solution(15281921034723681980)
XLA Ops:
  1.3 72.3 %layer_and_exchanges.1 = (bf16[4,2,4,8,16,256]{5,4,3,2,1,0:T(8,128)(2,1)}, f32[1024,128]{1,0:T(8,128)}, f32[8,128]{1,0:T(8,128)}) custom-call(f32[4,16]{1,0:T(4,128)} %bitcast.13, f32[4,32]{1,0:T(4,128)} %bitcast.14, s32[1,1]{1,0:T(1,128)} %bitcast.9.length_hbm, s32[1,256]{1,0:T(1,128)} %bitcast.15, s32[1,256]{1,0:T(1,128)} %local_hbm.1, s32[1,256]{1,0:T(1,128)} %deg_hbm.1, ...), custom_call_target="tpu_custom_call" | custom-call | tf_op jit(solution)/shard_map/layer_and_exchanges/pallas_call | solution.py:701
  73.6 4.0 %write_outputs.1 = (f32[1024,128]{1,0:T(8,128)}, f32[1024,256]{1,0:T(8,128)}, f32[1024,256]{1,0:T(8,128)}, f32[1024,256]{1,0:T(8,128)}, f32[256,1024]{1,0:T(8,128)}, /*index=5*/f32[4,16]{1,0:T(4,128)}, f32[4,32]{1,0:T(4,128)}) custom-call(bf16[4,1024,256]{2,1,0:T(8,128)(2,1)} %bitcast.10, f32[1024,128]{1,0:T(8,128)} %get-tuple-element.18.table_hbm, ...), custom_call_target="tpu_custom_call" | custom-call | tf_op jit(solution)/shard_map/write_outputs/pallas_call | solution.py:788

commit v5 on v4

--- a/solution.py
+++ b/solution.py
@@ -374,12 +374,16 @@
         x_give(c, 1, me_x, high, down)
         x_give(c, 2, me_x, high, up)
         x_give(c, 3, me_x, low, down)
+        if c == chunks - 1:
+            x_give(c, 4, me_x, pl.ds(0, n_z), across_x)
 
     def x_pass(c):
         wait_bytes(out_ref.at[c, 0, 0, low], xsem.at[0, c])
-        x_give(c, 4, down, low, up)
+        if c < chunks - 1:
+            x_give(c, 4, down, low, up)
         wait_bytes(out_ref.at[c, 0, 0, low], xsem.at[1, c])
-        x_give(c, 4, up, high, down)
+        if c < chunks - 1:
+            x_give(c, 4, up, high, down)
 
     def x_done(c):
         wait_bytes(out_ref.at[c, 0, 0, low], xsem.at[2, c])

time: 77.7 us -> 78.8 us (1.014)
  Pallas kernels: 76.2 us -> 77.4 us
    pallas_call x1, Pallas kernels: 72.3 us -> 73.4 us  [on_device(): pl.pallas_call(functools.partial(train_kernel, n_batch, n_node), out_shap...]
where the time goes in v5:
time: 78.8 us; the launch traced here: 78.7 us
  Pallas kernels  77.4 us (98%)
  between operations  1.29 us (2%)
    pallas_call x1, Pallas kernels, on_device(): pl.pallas_call(functools.partial(train_kernel, n_batch, n_node), out_shap...  73.4 us
    pallas_call x1, Pallas kernels, on_device(): pl.pallas_call(finish_kernel, out_shape=(shaped((table_rows, half), F32),...  3.97 us

profile of v5, /device:TPU:1, one launch (start us, length us, event | category | flops | bytes accessed | tf_op | source)
XLA Modules:
  0.0 78.7 jit_solution(890193334201310435)
XLA Ops:
  1.3 73.4 %layer_and_exchanges.1 = (bf16[4,2,4,8,16,256]{5,4,3,2,1,0:T(8,128)(2,1)}, f32[1024,128]{1,0:T(8,128)}, f32[8,128]{1,0:T(8,128)}) custom-call(f32[4,16]{1,0:T(4,128)} %bitcast.13, f32[4,32]{1,0:T(4,128)} %bitcast.14, s32[1,1]{1,0:T(1,128)} %bitcast.9.length_hbm, s32[1,256]{1,0:T(1,128)} %bitcast.15, s32[1,256]{1,0:T(1,128)} %local_hbm.1, s32[1,256]{1,0:T(1,128)} %deg_hbm.1, ...), custom_call_target="tpu_custom_call" | custom-call | tf_op jit(solution)/shard_map/layer_and_exchanges/pallas_call | solution.py:705
  74.7 4.0 %write_outputs.1 = (f32[1024,128]{1,0:T(8,128)}, f32[1024,256]{1,0:T(8,128)}, f32[1024,256]{1,0:T(8,128)}, f32[1024,256]{1,0:T(8,128)}, f32[256,1024]{1,0:T(8,128)}, /*index=5*/f32[4,16]{1,0:T(4,128)}, f32[4,32]{1,0:T(4,128)}) custom-call(bf16[4,1024,256]{2,1,0:T(8,128)(2,1)} %bitcast.10, f32[1024,128]{1,0:T(8,128)} %get-tuple-element.18.table_hbm, ...), custom_call_target="tpu_custom_call" | custom-call | tf_op jit(solution)/shard_map/write_outputs/pallas_call | solution.py:792
